TPU v7x, 32 devices: a whole 2x2x4 slice. The times are simulated.
32 devices in a mesh: row: 8 (over z, y), col: 4 (over x, core).
Axes of the slice: x: 2, y: 2, z: 4, core: 2. Of those that a mesh axis runs over, the one named last changes fastest.
Arguments:
- density: float32 [2, 160, 32, 160, 160], P(None, 'col', None, 'row'), may hold values from -2 to 2
- potential: float32 [160, 160], P('row'), may hold values from 0 to 2
Outputs:
- liouville: float32 [2, 160, 160, 1024], P(None, 'col', 'row')
All inputs are finite; a program needn't handle non-finite values.
Results may differ from a plain program's by a relative error of at most 0.000055.
Values sent between devices are 32-bit elements; how exact they have to be, the bound alone decides.
A program may use at most 384 MiB of HBM per device.

v0:
```python
import jax
import jax.numpy as jnp
from jax import lax
from jax.sharding import PartitionSpec as P

friction = 0.005
diffusion = 0.0001
highest = lax.Precision.HIGHEST


def operators(grid_width):
    positions = jnp.arange(grid_width)
    signed = jnp.where(positions < grid_width // 2, positions, positions - grid_width)
    wavenumber = 2.0 * jnp.pi / grid_width * signed.astype(jnp.float32)
    slope_wave = jnp.where(positions == grid_width // 2, 0.0, wavenumber)
    phases = positions[:, None] * positions[None, :] % grid_width
    angles = 2.0 * jnp.pi / grid_width * phases.astype(jnp.float32)
    kinetic_row = jnp.sum(0.5 * wavenumber * wavenumber * jnp.cos(angles), axis=1) / grid_width
    slope_row = -jnp.sum(slope_wave * jnp.sin(angles), axis=1) / grid_width
    distance = (positions[:, None] - positions[None, :]) % grid_width
    return (kinetic_row[distance], slope_row[distance])


def on_device(density, potential):
    grid_width = density.shape[4]
    window_size = density.shape[2]
    cols_here = density.shape[1]
    rows_here = density.shape[3]
    kinetic, slope_matrix = operators(grid_width)
    matrices = jnp.concatenate([kinetic[:window_size].T, slope_matrix[:window_size].T], axis=1)
    product = jnp.einsum("cpqbx,xe->cpebq", density, matrices, precision=highest)
    kinetic_one = product[:, :, :window_size]
    grad_one = product[:, :, window_size:]
    window_part = jnp.transpose(density[..., :window_size], (0, 1, 4, 3, 2))
    local_potential = potential[:, :window_size].T.reshape(1, 1, window_size, rows_here, 1)
    applied = kinetic_one + local_potential * window_part
    stacked = jnp.concatenate([kinetic, slope_matrix], axis=0)
    row_start = lax.axis_index("row") * rows_here
    col_start = lax.axis_index("col") * cols_here
    offset_one = (jnp.arange(window_size)[:, None] - jnp.arange(window_size)[None, :]).astype(
        jnp.float32
    )
    offset_one = offset_one.reshape(1, 1, window_size, 1, window_size)
    rows_global = (
        (row_start + jnp.arange(rows_here)).astype(jnp.float32).reshape(1, 1, 1, rows_here, 1)
    )
    cols_global = (
        (col_start + jnp.arange(cols_here)).astype(jnp.float32).reshape(1, cols_here, 1, 1, 1)
    )
    offset_two = rows_global - cols_global
    squared = offset_one**2 + offset_two**2
    source = lax.all_to_all(window_part, "row", split_axis=2, concat_axis=3, tiled=True)
    applied_mid = lax.all_to_all(applied, "row", split_axis=2, concat_axis=3, tiled=True)
    grad_mid = lax.all_to_all(grad_one, "row", split_axis=2, concat_axis=3, tiled=True)
    paired = jnp.einsum("capbq,eb->capeq", source, stacked, precision=highest)
    full_applied = applied_mid + paired[:, :, :, :grid_width]
    grad_two = paired[:, :, :, grid_width:]
    applied_back, grad_back = (
        lax.all_to_all(full_applied, "row", split_axis=3, concat_axis=2, tiled=True),
        lax.all_to_all(grad_two, "row", split_axis=3, concat_axis=2, tiled=True),
    )
    mirror_applied, mirror_one, mirror_two = (
        lax.all_to_all(
            lax.all_to_all(full_applied, "col", split_axis=3, concat_axis=1, tiled=True),
            "row",
            split_axis=1,
            concat_axis=2,
            tiled=True,
        ),
        lax.all_to_all(
            lax.all_to_all(grad_mid, "col", split_axis=3, concat_axis=1, tiled=True),
            "row",
            split_axis=1,
            concat_axis=2,
            tiled=True,
        ),
        lax.all_to_all(
            lax.all_to_all(grad_two, "col", split_axis=3, concat_axis=1, tiled=True),
            "row",
            split_axis=1,
            concat_axis=2,
            tiled=True,
        ),
    )
    mirror_applied = jnp.transpose(mirror_applied, (0, 3, 4, 1, 2))
    mirror_one = jnp.transpose(mirror_one, (0, 3, 4, 1, 2))
    mirror_two = jnp.transpose(mirror_two, (0, 3, 4, 1, 2))
    differ_real = applied_back[0] - mirror_applied[0]
    differ_imag = applied_back[1] + mirror_applied[1]
    first_real = grad_one[0] - mirror_one[0]
    first_imag = grad_one[1] + mirror_one[1]
    second_real = grad_back[0] - mirror_two[0]
    second_imag = grad_back[1] + mirror_two[1]
    real_out = differ_imag - friction * (offset_one[0] * first_real + offset_two[0] * second_real)
    imag_out = -differ_real - friction * (offset_one[0] * first_imag + offset_two[0] * second_imag)
    real_out = real_out - diffusion * squared[0] * window_part[0]
    imag_out = imag_out - diffusion * squared[0] * window_part[1]
    result = jnp.stack([real_out, imag_out])
    result = jnp.transpose(result, (0, 1, 3, 4, 2))
    return result.reshape(2, cols_here, rows_here, window_size * window_size)


def solution(mesh):
    in_specs = (P(None, "col", None, "row", None), P("row", None))
    out_specs = P(None, "col", "row", None)
    return jax.shard_map(
        on_device, mesh=mesh, in_specs=in_specs, out_specs=out_specs, check_vma=False
    )
```

profile of v0, /device:TPU:6, one launch (start us, length us, event | category | flops | bytes accessed | tf_op | source)
XLA Modules:
  0.0 2893.5 jit_solution(5164920676413358979)
XLA Ops:
  0.1 46.7 %copy.127 = f32[2,40,32,20,160]{4,1,3,2,0:T(8,128)} copy(f32[2,40,32,20,160]{4,2,3,1,0:T(8,128)} %param.2) | data formatting | bytes 65536000 | tf_op args[0]
  47.8 158.1 %gather_fusion.1 = f32[25600]{0:T(1024)S(1)} fusion(f32[160]{0:T(256)S(1)} %negate_multiply_fusion, s32[25600]{0:T(1024)S(1)} %broadcast_clamp_fusion), kind=kCustom, calls=%fused_computation.1 | custom fusion | bytes 307200 | tf_op jit(solution)/shard_map/gather | solution.py:21
  206.7 158.1 %gather_fusion = f32[25600]{0:T(1024)S(1)} fusion(f32[160]{0:T(256)S(1)} %broadcast_multiply_fusion, s32[25600]{0:T(1024)S(1)} %broadcast_clamp_fusion), kind=kCustom, calls=%fused_computation | custom fusion | bytes 307200 | tf_op jit(solution)/shard_map/gather | solution.py:21
  365.0 75.3 %convolution_bitcast_fusion = f32[2,40,64,20,32]{2,1,3,4,0:T(8,128)} fusion(f32[160,32]{0,1:T(8,128)S(1)} %bitcast.148, f32[160,32]{0,1:T(8,128)S(1)} %bitcast.149, f32[2,40,32,20,160]{4,2,3,1,0:T(8,128)} %param.2), kind=kOutput, calls=%fused_computation.10 | convolution fusion | flops 6291466240 | bytes 45916160 | tf_op jit(solution)/shard_map/cpqbx,xe->cpebq/dot_general | solution.py:31
  440.2 43.1 %slice_add_fusion = (f32[2,40,32,20,32]{2,1,3,4,0:T(8,128)}, f32[2,40,32,20,32]{2,1,3,4,0:T(8,128)}) fusion(f32[2,40,64,20,32]{2,1,3,4,0:T(8,128)} %convolution_bitcast_fusion, f32[32,20]{0,1:T(8,128)S(1)} %slice_bitcast_fusion.1, f32[2,40,32,20,160]{4,1,3,2,0:T(8,128)} %copy.127), kind=kLoop, calls=%fused_computation.3 | loop fusion | flops 3276800 | bytes 32770560 | tf_op jit(solution)/shard_map/add | solution.py:36
  483.3 24.2 copy.129
  507.5 23.1 reshape.236
  536.9 17.5 slice_bitcast_fusion
  554.4 24.1 copy.134
  578.5 23.0 reshape.222
  601.5 78.7 %all-to-all-done = f32[8,1,204800]{2,1,0:T(1,128)} async-done(((f32[8,1,204800]{2,1,0:T(1,128)}), f32[8,1,204800]{2,1,0:T(1,128)}, u32[]{:S(2)}, u32[]{:S(2)}) %all-to-all-start) | async-done | bytes 6553632 | tf_op jit(solution)/shard_map/all_to_all | solution.py:53
  685.4 24.1 copy.148
  709.5 23.0 reshape.230
  732.5 95.4 %all-to-all-done.1 = f32[8,1,204800]{2,1,0:T(1,128)} async-done(((f32[8,1,204800]{2,1,0:T(1,128)}), f32[8,1,204800]{2,1,0:T(1,128)}, u32[]{:S(2)}, u32[]{:S(2)}) %all-to-all-start.1) | async-done | bytes 6553632 | tf_op jit(solution)/shard_map/all_to_all | solution.py:52
  834.0 57.0 %reduce = f32[8,204800]{1,0:T(8,128)} reduce(f32[8,1,204800]{2,1,0:T(1,128)} %all-to-all-done, f32[]{:T(128)} %broadcast.227), dimensions={1}, to_apply=%all_to_all.139.reduce_sub_computation | reduce | bytes 13107204 | tf_op jit(solution)/shard_map/all_to_all | solution.py:53
  891.0 26.9 reshape.237
  917.9 16.9 copy.131
  934.8 19.5 copy.138
  954.4 57.0 %reduce.1 = f32[8,204800]{1,0:T(8,128)} reduce(f32[8,1,204800]{2,1,0:T(1,128)} %all-to-all-done.1, f32[]{:T(128)} %broadcast.227), dimensions={1}, to_apply=%all_to_all.143.reduce_sub_computation | reduce | bytes 13107204 | tf_op jit(solution)/shard_map/all_to_all | solution.py:52
  1011.3 26.9 reshape.223
  1048.3 43.6 %fusion.15 = f32[2,40,4,320,32]{3,1,4,2,0:T(8,128)} fusion(f32[2,40,4,160,32]{1,4,3,2,0:T(8,128)S(1)} %bitcast.113, f32[160,160]{0,1:T(8,128)S(1)} %copy.133, f32[160,160]{0,1:T(8,128)S(1)} %copy.132), kind=kOutput, calls=%fused_computation.34 | convolution fusion | flops 6291507200 | bytes 19865600 | tf_op jit(solution)/shard_map/capbq,eb->capeq/dot_general | solution.py:55
  1108.7 18.5 copy.156
  1127.2 33.5 %reshape.226 = f32[4,1,409600]{2,1,0:T(1,128)} reshape(f32[160,2,4,32,40]{4,3,2,1,0:T(8,128)} %bitcast.109) | data formatting | bytes 13107200
  1166.6 56.9 %reduce.5 = f32[8,204800]{1,0:T(8,128)} reduce(f32[8,1,204800]{2,1,0:T(1,128)} %all-to-all-done.5, f32[]{:T(128)} %broadcast.227), dimensions={1}, to_apply=%all_to_all.158.reduce_sub_computation | reduce | bytes 13107204 | tf_op jit(solution)/shard_map/all_to_all | solution.py:54
  1223.4 26.9 reshape.231
  1267.6 33.5 %reshape.232 = f32[4,1,409600]{2,1,0:T(1,128)} reshape(f32[160,2,4,32,40]{4,3,2,1,0:T(8,128)} %bitcast.126) | data formatting | bytes 13107200
  1306.5 18.6 copy.139
  1325.1 33.3 %reshape.240 = f32[4,1,409600]{2,1,0:T(1,128)} reshape(f32[160,2,4,32,40]{4,3,2,1,0:T(8,128)} %bitcast.111) | data formatting | bytes 13107200
  1358.5 19.9 all-to-all-done.6
  1385.3 22.9 reshape.224
  1408.3 49.0 %all-to-all-done.3 = f32[4,1,409600]{2,1,0:T(1,128)} async-done(((f32[4,1,409600]{2,1,0:T(1,128)}), f32[4,1,409600]{2,1,0:T(1,128)}, u32[]{:S(2)}, u32[]{:S(2)}) %all-to-all-start.3) | async-done | bytes 6553632 | tf_op jit(solution)/shard_map/all_to_all | solution.py:64
  1463.2 22.9 reshape.238
  1486.2 120.4 %all-to-all-done.8 = f32[8,1,204800]{2,1,0:T(1,128)} async-done(((f32[8,1,204800]{2,1,0:T(1,128)}), f32[8,1,204800]{2,1,0:T(1,128)}, u32[]{:S(2)}, u32[]{:S(2)}) %all-to-all-start.8) | async-done | bytes 6553632 | tf_op jit(solution)/shard_map/all_to_all | solution.py:60
  1612.3 71.4 %reduce.3 = f32[4,409600]{1,0:T(4,128)} reduce(f32[4,1,409600]{2,1,0:T(1,128)} %all-to-all-done.9, f32[]{:T(128)} %broadcast.227), dimensions={1}, to_apply=%all_to_all.173.reduce_sub_computation | reduce | bytes 13107204 | tf_op jit(solution)/shard_map/all_to_all | solution.py:78
  1683.7 27.3 reshape.227
  1711.0 25.6 copy.191
  1736.6 30.3 %copy.179 = f32[2,4,40,4,40,32]{4,5,3,0,2,1:T(8,128)} copy(f32[2,4,40,4,40,32]{2,1,5,4,3,0:T(4,128)} %bitcast.128) | data formatting | bytes 13107200 | tf_op jit(solution)/shard_map/all_to_all | solution.py:78
  1766.8 22.9 reshape.228
  1795.8 71.7 %reduce.6 = f32[4,409600]{1,0:T(4,128)} reduce(f32[4,1,409600]{2,1,0:T(1,128)} %all-to-all-done.6, f32[]{:T(128)} %broadcast.227), dimensions={1}, to_apply=%all_to_all.162.reduce_sub_computation | reduce | bytes 13107204 | tf_op jit(solution)/shard_map/all_to_all | solution.py:71
  1867.5 27.3 reshape.233
  1894.8 25.6 copy.192
  1920.4 30.2 %copy.177 = f32[2,4,40,4,40,32]{4,5,3,0,2,1:T(8,128)} copy(f32[2,4,40,4,40,32]{2,1,5,4,3,0:T(4,128)} %bitcast.131) | data formatting | bytes 13107200 | tf_op jit(solution)/shard_map/all_to_all | solution.py:71
  1950.6 23.0 reshape.234
  1979.6 71.8 %reduce.9 = f32[4,409600]{1,0:T(4,128)} reduce(f32[4,1,409600]{2,1,0:T(1,128)} %all-to-all-done.3, f32[]{:T(128)} %broadcast.227), dimensions={1}, to_apply=%all_to_all.150.reduce_sub_computation | reduce | bytes 13107204 | tf_op jit(solution)/shard_map/all_to_all | solution.py:64
  2051.4 27.3 reshape.241
  2078.6 25.6 copy.193
  2104.2 30.3 %copy.174 = f32[2,4,40,4,40,32]{4,5,3,0,2,1:T(8,128)} copy(f32[2,4,40,4,40,32]{2,1,5,4,3,0:T(4,128)} %bitcast.134) | data formatting | bytes 13107200 | tf_op jit(solution)/shard_map/all_to_all | solution.py:64
  2134.5 23.0 reshape.242
  2165.3 57.2 %reduce.2 = f32[8,204800]{1,0:T(8,128)} reduce(f32[8,1,204800]{2,1,0:T(1,128)} %all-to-all-done.8, f32[]{:T(128)} %broadcast.227), dimensions={1}, to_apply=%all_to_all.170.reduce_sub_computation | reduce | bytes 13107204 | tf_op jit(solution)/shard_map/all_to_all | solution.py:60
  2222.5 26.7 reshape.225
  2288.9 57.2 %reduce.8 = f32[8,204800]{1,0:T(8,128)} reduce(f32[8,1,204800]{2,1,0:T(1,128)} %all-to-all-done.2, f32[]{:T(128)} %broadcast.227), dimensions={1}, to_apply=%all_to_all.147.reduce_sub_computation | reduce | bytes 13107204 | tf_op jit(solution)/shard_map/all_to_all | solution.py:59
  2346.1 26.7 reshape.239
  2457.1 57.0 %reduce.4 = f32[8,204800]{1,0:T(8,128)} reduce(f32[8,1,204800]{2,1,0:T(1,128)} %all-to-all-done.10, f32[]{:T(128)} %broadcast.227), dimensions={1}, to_apply=%all_to_all.177.reduce_sub_computation | reduce | bytes 13107204 | tf_op jit(solution)/shard_map/all_to_all | solution.py:77
  2514.1 27.0 reshape.229
  2541.1 23.6 copy.163
  2564.6 57.0 %reduce.7 = f32[8,204800]{1,0:T(8,128)} reduce(f32[8,1,204800]{2,1,0:T(1,128)} %all-to-all-done.7, f32[]{:T(128)} %broadcast.227), dimensions={1}, to_apply=%all_to_all.166.reduce_sub_computation | reduce | bytes 13107204 | tf_op jit(solution)/shard_map/all_to_all | solution.py:70
  2621.6 26.8 reshape.235
  2648.4 23.5 copy.155
  2671.9 57.2 %reduce.10 = f32[8,204800]{1,0:T(8,128)} reduce(f32[8,1,204800]{2,1,0:T(1,128)} %all-to-all-done.4, f32[]{:T(128)} %broadcast.227), dimensions={1}, to_apply=%all_to_all.154.reduce_sub_computation | reduce | bytes 13107204 | tf_op jit(solution)/shard_map/all_to_all | solution.py:63
  2729.1 26.7 reshape.243
  2755.8 23.6 copy.146
  2779.4 65.5 %fusion.9 = (f32[1,40,32,20,32]{2,1,3,4,0:T(8,128)}, f32[1,40,32,20,32]{2,1,3,4,0:T(8,128)}) fusion(f32[2,40,32,20,32]{2,1,3,4,0:T(8,128)} %slice_bitcast_fusion, f32[1,40,32,20,32]{2,1,3,4,0:T(8,128)} %copy.164, f32[2,40,32,20,32]{2,1,3,4,0:T(8,128)} %bitcast.114, f32[2,40,32,20,32]{2,1,3,4,0:T(8,128)} %bitcast.115, ...), kind=kLoop, calls=%fused_computation.23 | loop fusion | flops 18841600 | bytes 52443392 | tf_op jit(solution)/shard_map/sub | solution.py:96
  2855.1 17.6 copy.169
  2872.7 20.6 reshape.199
  (83 shorter events, 247.9 us)
Async XLA Ops:
  205.9 159.0 %copy-start = (f32[25600]{0:T(1024)}, f32[25600]{0:T(1024)S(1)}, u32[]{:S(2)}) copy-start(f32[25600]{0:T(1024)S(1)} %gather_fusion.1) | copy-start | bytes 307204
  206.7 158.2 %copy-start.8 = (f32[20,160]{1,0:T(8,128)S(1)}, f32[20,160]{1,0:T(8,128)}, u32[]{:S(2)}) copy-start(f32[20,160]{1,0:T(8,128)} %param.3) | copy-start | bytes 38404
  364.8 75.4 %copy-start.2 = (f32[25600]{0:T(1024)}, f32[25600]{0:T(1024)S(1)}, u32[]{:S(2)}) copy-start(f32[25600]{0:T(1024)S(1)} %gather_fusion) | copy-start | bytes 307204
  530.6 149.6 %all-to-all-start = ((f32[8,1,204800]{2,1,0:T(1,128)}), f32[8,1,204800]{2,1,0:T(1,128)}, u32[]{:S(2)}, u32[]{:S(2)}) async-start(f32[8,1,204800]{2,1,0:T(1,128)} %reshape.236), calls=%async_computation | async-start | bytes 13107200 | tf_op jit(solution)/shard_map/all_to_all | solution.py:53
  680.2 147.7 %all-to-all-start.1 = ((f32[8,1,204800]{2,1,0:T(1,128)}), f32[8,1,204800]{2,1,0:T(1,128)}, u32[]{:S(2)}, u32[]{:S(2)}) async-start(f32[8,1,204800]{2,1,0:T(1,128)} %reshape.222), calls=%async_computation.1 | async-start | bytes 13107200 | tf_op jit(solution)/shard_map/all_to_all | solution.py:52
  732.5 100.6 %copy-start.1 = (f32[25600]{0:T(1024)S(1)}, f32[25600]{0:T(1024)}, u32[]{:S(2)}) copy-start(f32[25600]{0:T(1024)} %copy-done) | copy-start | bytes 307204
  732.5 100.7 %copy-start.3 = (f32[25600]{0:T(1024)S(1)}, f32[25600]{0:T(1024)}, u32[]{:S(2)}) copy-start(f32[25600]{0:T(1024)} %copy-done.2) | copy-start | bytes 307204
  827.9 332.9 %all-to-all-start.5 = ((f32[8,1,204800]{2,1,0:T(1,128)}), f32[8,1,204800]{2,1,0:T(1,128)}, u32[]{:S(2)}, u32[]{:S(2)}) async-start(f32[8,1,204800]{2,1,0:T(1,128)} %reshape.230), calls=%async_computation.5 | async-start | bytes 13107200 | tf_op jit(solution)/shard_map/all_to_all | solution.py:54
  1038.2 53.7 %slice-start = ((s8[10485760]{0:T(1024)(128)(4,1)}), s8[4194304]{0:T(1024)(128)(4,1)S(1)}, s32[]{:S(2)}) async-start(s8[10485760]{0:T(1024)(128)(4,1)} %bitcast.146), calls=%async_computation.11 | async-start | bytes 8388608
  1038.2 53.7 %slice-start.1 = ((s8[10485760]{0:T(1024)(128)(4,1)}), s8[4194304]{0:T(1024)(128)(4,1)S(1)}, s32[]{:S(2)}) async-start(s8[10485760]{0:T(1024)(128)(4,1)} %bitcast.146), calls=%async_computation.12 | async-start | bytes 8388608
  1048.3 43.6 %slice-start.2 = ((s8[10485760]{0:T(1024)(128)(4,1)}), s8[2097152]{0:T(1024)(128)(4,1)S(1)}, s32[]{:S(2)}) async-start(s8[10485760]{0:T(1024)(128)(4,1)} %bitcast.146), calls=%async_computation.13 | async-start | bytes 4194304
  1160.7 140.3 %all-to-all-start.9 = ((f32[4,1,409600]{2,1,0:T(1,128)}), f32[4,1,409600]{2,1,0:T(1,128)}, u32[]{:S(2)}, u32[]{:S(2)}) async-start(f32[4,1,409600]{2,1,0:T(1,128)} %reshape.226), calls=%async_computation.9 | async-start | bytes 13107200 | tf_op jit(solution)/shard_map/all_to_all | solution.py:78
  1301.0 77.3 %all-to-all-start.6 = ((f32[4,1,409600]{2,1,0:T(1,128)}), f32[4,1,409600]{2,1,0:T(1,128)}, u32[]{:S(2)}, u32[]{:S(2)}) async-start(f32[4,1,409600]{2,1,0:T(1,128)} %reshape.232), calls=%async_computation.6 | async-start | bytes 13107200 | tf_op jit(solution)/shard_map/all_to_all | solution.py:71
  1378.3 78.9 %all-to-all-start.3 = ((f32[4,1,409600]{2,1,0:T(1,128)}), f32[4,1,409600]{2,1,0:T(1,128)}, u32[]{:S(2)}, u32[]{:S(2)}) async-start(f32[4,1,409600]{2,1,0:T(1,128)} %reshape.240), calls=%async_computation.3 | async-start | bytes 13107200 | tf_op jit(solution)/shard_map/all_to_all | solution.py:64
  1457.2 149.4 %all-to-all-start.8 = ((f32[8,1,204800]{2,1,0:T(1,128)}), f32[8,1,204800]{2,1,0:T(1,128)}, u32[]{:S(2)}, u32[]{:S(2)}) async-start(f32[8,1,204800]{2,1,0:T(1,128)} %reshape.224), calls=%async_computation.8 | async-start | bytes 13107200 | tf_op jit(solution)/shard_map/all_to_all | solution.py:60
  1606.6 183.2 %all-to-all-start.2 = ((f32[8,1,204800]{2,1,0:T(1,128)}), f32[8,1,204800]{2,1,0:T(1,128)}, u32[]{:S(2)}, u32[]{:S(2)}) async-start(f32[8,1,204800]{2,1,0:T(1,128)} %reshape.238), calls=%async_computation.2 | async-start | bytes 13107200 | tf_op jit(solution)/shard_map/all_to_all | solution.py:59
  1789.8 183.8 %all-to-all-start.10 = ((f32[8,1,204800]{2,1,0:T(1,128)}), f32[8,1,204800]{2,1,0:T(1,128)}, u32[]{:S(2)}, u32[]{:S(2)}) async-start(f32[8,1,204800]{2,1,0:T(1,128)} %reshape.228), calls=%async_computation.10 | async-start | bytes 13107200 | tf_op jit(solution)/shard_map/all_to_all | solution.py:77
  1973.6 183.9 %all-to-all-start.7 = ((f32[8,1,204800]{2,1,0:T(1,128)}), f32[8,1,204800]{2,1,0:T(1,128)}, u32[]{:S(2)}, u32[]{:S(2)}) async-start(f32[8,1,204800]{2,1,0:T(1,128)} %reshape.234), calls=%async_computation.7 | async-start | bytes 13107200 | tf_op jit(solution)/shard_map/all_to_all | solution.py:70
  2157.4 514.5 %all-to-all-start.4 = ((f32[8,1,204800]{2,1,0:T(1,128)}), f32[8,1,204800]{2,1,0:T(1,128)}, u32[]{:S(2)}, u32[]{:S(2)}) async-start(f32[8,1,204800]{2,1,0:T(1,128)} %reshape.242), calls=%async_computation.4 | async-start | bytes 13107200 | tf_op jit(solution)/shard_map/all_to_all | solution.py:63
  2755.8 23.6 copy-start.4
  2755.8 23.6 copy-start.5
  2755.8 23.6 copy-start.6
  2755.8 23.6 copy-start.7
where the time goes:
time: 2910 us; the launch traced here: 2890 us
  local copies, waits for them, and re-layouts  1540 us (53%)
  other arithmetic  810 us (28%)
  waiting for transfers between devices  363 us (12%)
  matrix products  119 us (4%)
  starting transfers between devices  64.8 us (2%)
    unnamed x47, local copies, waits for them, and re-layouts  627 us
    gather x6, local copies, waits for them, and re-layouts, operators(): return (kinetic_row[distance], slope_row[distance])  317 us
    all_to_all x1, waiting for transfers between devices, on_device(): lax.all_to_all(grad_two, 'row', split_axis=3, concat_axis=2, tiled=True)  120 us
    all_to_all x1, waiting for transfers between devices, on_device(): lax.all_to_all(window_part, 'row', split_axis=2, concat_axis=3, tiled=True)  95.4 us
    all_to_all x1, waiting for transfers between devices, on_device(): lax.all_to_all(applied, 'row', split_axis=2, concat_axis=3, tiled=True)  78.7 us
    dot_general x1, matrix products, on_device(): jnp.einsum('cpqbx,xe->cpebq', density, matrices, precision=highest)  75.3 us
    all_to_all x1, other arithmetic, on_device(): lax.all_to_all(full_applied, 'col', split_axis=3, concat_axis=1, tiled=True)  71.8 us
    all_to_all x1, other arithmetic, on_device(): lax.all_to_all(grad_mid, 'col', split_axis=3, concat_axis=1, tiled=True)  71.7 us
  transfers between devices with their start and end apart: 11, of which 5 were waited for; matrix products, arithmetic and copies ran while one was open for 59% of the time, Pallas kernels for 0%

commit v1 on v0

v1 whole, which is shorter than its diff:
```python
import functools

import jax
import jax.numpy as jnp
import numpy as np
from jax import lax
from jax.experimental import pallas as pl
from jax.experimental.pallas import tpu as pltpu
from jax.sharding import PartitionSpec as P

friction = 0.005
diffusion = 0.0001
LANES = 128
VMEM = 56 * 2**20


def operators(grid_width):
    n = np.arange(grid_width)
    wave = 2.0 * np.pi * np.fft.fftfreq(grid_width)
    slope_wave = np.where(n == grid_width // 2, 0.0, wave)
    angles = 2.0 * np.pi / grid_width * (n[:, None] * n[None, :] % grid_width)
    kinetic_row = (0.5 * wave * wave * np.cos(angles)).sum(1) / grid_width
    slope_row = -(slope_wave * np.sin(angles)).sum(1) / grid_width
    distance = (n[:, None] - n[None, :]) % grid_width
    return kinetic_row[distance], slope_row[distance]


def split_host(matrix):
    high = matrix.astype(np.float32).astype(jnp.bfloat16)
    low = (matrix - high.astype(np.float64)).astype(np.float32).astype(jnp.bfloat16)
    return jnp.asarray(high), jnp.asarray(low)


def split(values):
    high = values.astype(jnp.bfloat16)
    return high, (values - high.astype(jnp.float32)).astype(jnp.bfloat16)


def dot(a, b):
    return jnp.dot(a, b, preferred_element_type=jnp.float32)


def up8(n):
    return (n + 7) // 8 * 8


def first_kernel(group, rows, d_ref, v_ref, high_ref, low_ref, eye_ref, w_ref, l_ref, pad):
    blocks, tall = pad.shape[0], pad.shape[1]

    @pl.when((pl.program_id(0) == 0) & (pl.program_id(1) == 0))
    def _():
        pad[...] = jnp.zeros_like(pad)

    window, mixed = [], []
    for c in range(2):
        win = jnp.zeros((blocks * tall, LANES), jnp.float32)
        mix = jnp.zeros((blocks * tall, 2 * LANES), jnp.float32)
        for q in range(group):
            pad[:, :rows, :] = d_ref[c, :, q]
            high, low = split(pad[...].reshape(blocks * tall, pad.shape[2]))
            mix += dot(high, high_ref[q]) + dot(low, high_ref[q]) + dot(high, low_ref[q])
            win += dot(high, eye_ref[q]) + dot(low, eye_ref[q])
        window.append(win.reshape(blocks, tall, LANES)[:, :rows])
        mixed.append(mix.reshape(blocks, tall, 2 * LANES)[:, :rows])
    v = v_ref[...][None]
    w_ref[0, 0] = window[0]
    w_ref[0, 1] = window[1]
    l_ref[0] = mixed[1][..., :LANES] + mixed[0][..., LANES:] + v * window[1]
    l_ref[1] = mixed[1][..., LANES:] - mixed[0][..., :LANES] - v * window[0]


def mirror_kernel(rows, l_ref, perm_ref, o_ref, pad, back):
    sign = 1.0 - 2.0 * pl.program_id(0).astype(jnp.float32)
    tall, lanes = pad.shape[1], pad.shape[2]
    quarters, wide = o_ref.shape[0], o_ref.shape[5]
    pad[...] = jnp.zeros_like(pad)
    for b in range(rows):
        pad[b, :rows, :] = l_ref[0, :, b, :]
    high, low = split(pad[...].reshape(rows * tall, lanes) * sign)
    for u in range(quarters):
        part = perm_ref[:, u * wide : (u + 1) * wide]
        out = dot(high, part) + dot(low, part)
        o_ref[u, 0, 0] = out.reshape(rows, tall, wide)[:, :rows]


def second_kernel(pieces, rows, tall, start_ref, *refs):
    parts = refs[:pieces]
    high_ref, low_ref, o_ref, pad = refs[pieces:]
    wide = pad.shape[2]

    @pl.when(pl.program_id(0) == 0)
    def _():
        pad[...] = jnp.zeros_like(pad)

    column = (start_ref[0] + pl.program_id(0)).astype(jnp.float32)
    out = []
    for c in range(2):
        for k in range(pieces):
            pad[c, k * tall : k * tall + rows, :] = parts[k][c, 0]
        high, low = split(pad[c])
        out.append(dot(high_ref[...], high) + dot(high_ref[...], low) + dot(low_ref[...], high))
    half = pieces * tall
    at = lax.broadcasted_iota(jnp.int32, (tall, wide), 0).astype(jnp.float32) - column
    for r in range(pieces):
        here = slice(r * tall, (r + 1) * tall)
        there = slice(half + r * tall, half + (r + 1) * tall)
        offset = friction * (at + float(r * rows))
        o_ref[r, 0, 0] = (out[1][here] - offset * out[0][there])[:rows]
        o_ref[r, 1, 0] = (-out[0][here] - offset * out[1][there])[:rows]


def last_kernel(quarters, ratio, rows, window, where_ref, y_ref, r_ref, w_ref, perm_ref, sq_ref, o_ref, pad):
    c, h = pl.program_id(0), pl.program_id(1)
    col, source, own, row_start, col_start = (where_ref[k] for k in range(5))
    sign = 1.0 - 2.0 * c.astype(jnp.float32)
    tall, wide = pad.shape[1], pad.shape[2]
    lanes = o_ref.shape[3]
    pad[...] = jnp.zeros_like(pad)
    total = jnp.zeros((rows * tall, lanes), jnp.float32)
    for u in range(quarters):
        s = lax.rem(col - u + quarters, quarters)
        for p in range(rows):
            pad[p, :rows, :] = y_ref[s, 0, 0, :, p, :]
        high, low = split(pad[...].reshape(rows * tall, wide) * sign)
        part = perm_ref[u * wide : (u + 1) * wide, :]
        total += dot(high, part) + dot(low, part)
    total = total.reshape(rows, tall, lanes)[:, :rows]
    b = row_start + lax.broadcasted_iota(jnp.int32, (rows, rows, 1), 1)
    p = col_start + h * rows + lax.broadcasted_iota(jnp.int32, (rows, rows, 1), 0)
    off2 = (b - p).astype(jnp.float32)
    off2 = off2 * off2
    j = lax.rem(own - h + ratio, ratio)
    for u in range(quarters):
        s = lax.rem(source - u + quarters, quarters)
        cut = slice(u * wide, (u + 1) * wide)
        squared = off2 + sq_ref[0, cut][None, None]
        o_ref[0, :, :, cut] = total[:, :, cut] + r_ref[s, j, 0] - diffusion * squared * w_ref[u, 0]


def params():
    return pltpu.CompilerParams(vmem_limit_bytes=VMEM)


def on_device(n_row, n_col, density, potential):
    width, window = density.shape[4], density.shape[2]
    cols, rows = density.shape[1], density.shape[3]
    ratio = n_row // n_col
    tall = up8(rows)
    lanes = window * window
    group = LANES // window
    groups = window // group
    quarters = n_col
    wide = lanes // quarters
    row, col = lax.axis_index("row"), lax.axis_index("col")
    zone, own = row // ratio, row % ratio
    kinetic, slope = operators(width)
    f32 = jnp.float32

    weights = np.zeros((window, width, 2 * LANES))
    eyes = np.zeros((group, width, LANES))
    e = np.arange(window)
    for q in range(window):
        at = (q % group) * window
        weights[q, :, at : at + window] = kinetic[:window].T
        weights[q, :, LANES + at : LANES + at + window] = -friction * (e - q)[None, :] * slope[:window].T
        if q < group:
            eyes[q, e, at + e] = 1.0
    whigh, wlow = split_host(weights)
    eye = jnp.asarray(eyes.astype(jnp.bfloat16))
    tiled = jnp.tile(potential[:, :window], (1, group))

    per = max(1, LANES // wide)
    unit = min(wide, LANES)
    store = max(wide, LANES)
    stores = lanes // store
    inner = store // LANES
    w_all, l_all = pl.pallas_call(
        functools.partial(first_kernel, group, rows),
        grid=(ratio, groups),
        in_specs=[
            pl.BlockSpec((2, rows, group, rows, width), lambda h, m: (0, h, m, 0, 0)),
            pl.BlockSpec((rows, LANES), lambda h, m: (0, 0)),
            pl.BlockSpec((group, width, 2 * LANES), lambda h, m: (m, 0, 0)),
            pl.BlockSpec((group, width, 2 * LANES), lambda h, m: (m, 0, 0)),
            pl.BlockSpec((group, width, LANES), lambda h, m: (0, 0, 0)),
        ],
        out_specs=[
            pl.BlockSpec((1, 2, rows, rows, LANES), lambda h, m: (m // inner, 0, h, 0, m % inner)),
            pl.BlockSpec((2, rows, rows, LANES), lambda h, m: (0, h, 0, m)),
        ],
        out_shape=[
            jax.ShapeDtypeStruct((stores, 2, cols, rows, store), f32),
            jax.ShapeDtypeStruct((2, cols, rows, lanes), f32),
        ],
        scratch_shapes=[pltpu.VMEM((rows, tall, width), f32)],
        compiler_params=params(),
        cost_estimate=pl.CostEstimate(flops=2 * 10**10, bytes_accessed=80 * 10**6, transcendentals=0),
        name="first_dimension",
    )(density, tiled, whigh, wlow, eye)
    if per > 1:
        w_all = jnp.moveaxis(w_all.reshape(stores, 2, cols, rows, per, wide), 4, 1).reshape(quarters, 2, cols, rows, wide)

    def permute(values, target):
        pairs = [(r * n_col + c, target(r, c)) for r in range(n_row) for c in range(n_col)]
        return lax.ppermute(values, ("row", "col"), pairs)

    def to_middle(j, k):
        return lambda r, c: (c * ratio + (r % ratio + j) % ratio) * n_col + (r // ratio + k) % n_col

    received = []
    for k in range(n_col):
        for j in range(ratio):
            piece = lax.dynamic_slice(
                w_all,
                ((zone + k) % n_col, 0, (own + j) % ratio * rows, 0, 0),
                (1, 2, rows, rows, wide),
            )[0]
            received.append(permute(piece, to_middle(j, k)))

    order = np.arange(lanes)
    perm = np.zeros((lanes, lanes), np.float32)
    perm[order, order % window * window + order // window] = 1.0
    perm = jnp.asarray(perm.astype(jnp.bfloat16))
    l_mirror = pl.pallas_call(
        functools.partial(mirror_kernel, rows),
        grid=(2, ratio),
        in_specs=[
            pl.BlockSpec((1, rows, rows, lanes), lambda c, h: (c, h, 0, 0)),
            pl.BlockSpec((lanes, lanes), lambda c, h: (0, 0)),
        ],
        out_specs=pl.BlockSpec((quarters, 1, 1, rows, rows, wide), lambda c, h: (0, h, c, 0, 0, 0)),
        out_shape=jax.ShapeDtypeStruct((quarters, ratio, 2, rows, rows, wide), f32),
        scratch_shapes=[pltpu.VMEM((rows, tall, lanes), f32), pltpu.VMEM((8, 128), f32)],
        compiler_params=params(),
        cost_estimate=pl.CostEstimate(flops=2 * 10**10, bytes_accessed=16 * 10**6, transcendentals=0),
        name="mirror_first",
    )(l_all, perm)

    pieces = n_row
    blocks = np.zeros((pieces, tall, 2, pieces, tall))
    for t, m in enumerate((kinetic, slope)):
        cut = m.reshape(pieces, rows, pieces, rows)
        blocks[:, :rows, t, :, :rows] = cut.transpose(2, 3, 0, 1)
    mhigh, mlow = split_host(blocks.reshape(pieces, tall, 2 * pieces * tall))
    sources = [
        (col - k + n_col) % n_col * ratio + (own - j + ratio) % ratio
        for k in range(n_col)
        for j in range(ratio)
    ]

    def arrange(m):
        picked = [lax.dynamic_index_in_dim(m, s, 0, keepdims=False) for s in sources]
        return jnp.concatenate(picked, axis=0).T

    l_second = pl.pallas_call(
        functools.partial(second_kernel, pieces, rows, tall),
        grid=(rows,),
        in_specs=[pl.BlockSpec(memory_space=pltpu.SMEM)]
        + [pl.BlockSpec((2, 1, rows, wide), lambda p: (0, p, 0, 0))] * pieces
        + [pl.BlockSpec((2 * pieces * tall, pieces * tall), lambda p: (0, 0))] * 2,
        out_specs=pl.BlockSpec((pieces, 2, 1, rows, wide), lambda p: (0, 0, p, 0, 0)),
        out_shape=jax.ShapeDtypeStruct((pieces, 2, rows, rows, wide), f32),
        scratch_shapes=[pltpu.VMEM((2, pieces * tall, wide), f32)],
        compiler_params=params(),
        name="second_dimension",
    )((row * rows).astype(jnp.int32).reshape(1), *received, arrange(mhigh), arrange(mlow))

    mine, arrived = [], []
    for s in range(n_col):
        piece = lax.dynamic_slice_in_dim(l_second, (col + s) % n_col * ratio, ratio, 0)
        if s > 0:
            piece = permute(piece, lambda r, c, s=s: r * n_col + (c + s) % n_col)
        half = piece + lax.dynamic_index_in_dim(l_mirror, (col - s + n_col) % n_col, 0, keepdims=False)
        mine.append(half)
        for j in range(ratio):
            out = lax.dynamic_index_in_dim(half, (own + j) % ratio, 0, keepdims=False)
            arrived.append(
                permute(out, lambda r, c, j=j: (c * ratio + (r % ratio + j) % ratio) * n_col + r // ratio)
            )
    mine = jnp.stack(mine)
    arrived = jnp.stack(arrived).reshape(n_col, ratio, 2, rows, rows, wide)

    where = jnp.stack([col, zone, own, row * rows, col * cols]).astype(jnp.int32)
    sq = ((order % window - order // window) ** 2).astype(np.float32).reshape(1, lanes)
    out = pl.pallas_call(
        functools.partial(last_kernel, quarters, ratio, rows, window),
        grid=(2, ratio),
        in_specs=[
            pl.BlockSpec(memory_space=pltpu.SMEM),
            pl.BlockSpec((n_col, 1, 1, rows, rows, wide), lambda c, h: (0, h, c, 0, 0, 0)),
            pl.BlockSpec((n_col, ratio, 1, rows, rows, wide), lambda c, h: (0, 0, c, 0, 0, 0)),
            pl.BlockSpec((quarters, 1, rows, rows, wide), lambda c, h: (0, c, h, 0, 0)),
            pl.BlockSpec((lanes, lanes), lambda c, h: (0, 0)),
            pl.BlockSpec((1, lanes), lambda c, h: (0, 0)),
        ],
        out_specs=pl.BlockSpec((1, rows, rows, lanes), lambda c, h: (c, h, 0, 0)),
        out_shape=jax.ShapeDtypeStruct((2, cols, rows, lanes), f32),
        scratch_shapes=[pltpu.VMEM((rows, tall, wide), f32)],
        compiler_params=params(),
        name="combine",
    )(where, mine, arrived, w_all, perm, jnp.asarray(sq))
    return out


def solution(mesh):
    body = functools.partial(on_device, mesh.shape["row"], mesh.shape["col"])
    in_specs = (P(None, "col", None, "row", None), P("row", None))
    out_specs = P(None, "col", "row", None)
    return jax.shard_map(
        body, mesh=mesh, in_specs=in_specs, out_specs=out_specs, check_vma=False
    )
```

time: 2910 us -> 803 us (0.28)
  local copies, waits for them, and re-layouts: 1540 us -> 121 us
  other arithmetic: 810 us -> 13.1 us
  matrix products: 119 us -> 0 us
  Pallas kernels: 0 us -> 101 us
  starting transfers between devices: 64.8 us -> 165 us
    all_to_all x11 -> x0, other arithmetic: 671 us -> none  [the longest x1 71.8 us: on_device(): lax.all_to_all(full_applied, 'col', split_axis=3, concat_axis=1, tiled=True)]
    unnamed x47 -> x10, local copies, waits for them, and re-layouts: 627 us -> 57.9 us
    ppermute x0 -> x19, waiting for transfers between devices: none -> 392 us  [permute(): return lax.ppermute(values, ('row', 'col'), pairs)]
    all_to_all x11 -> x0, waiting for transfers between devices: 363 us -> none  [the longest x1 120 us: on_device(): lax.all_to_all(grad_two, 'row', split_axis=3, concat_axis=2, tiled=True)]
    all_to_all x17 -> x0, local copies, waits for them, and re-layouts: 320 us -> none  [the longest x2 55.8 us: on_device(): lax.all_to_all(grad_two, 'col', split_axis=3, concat_axis=1, tiled=True)]
    gather x6 -> x0, local copies, waits for them, and re-layouts: 317 us -> none  [operators(): return (kinetic_row[distance], slope_row[distance])]
    ppermute x0 -> x19, starting transfers between devices: none -> 165 us  [permute(): return lax.ppermute(values, ('row', 'col'), pairs)]
    dot_general x2 -> x0, matrix products: 119 us -> none  [the longest x1 75.3 us: on_device(): jnp.einsum('cpqbx,xe->cpebq', density, matrices, precision=highest)]
  transfers between devices with their start and end apart: 11 -> 19, of which waited for: 5 -> 10; matrix products, arithmetic and copies ran while one was open for 59% -> 6% of each run, Pallas kernels for 0% -> 2%
where the time goes in v1:
time: 803 us; the launch traced here: 793 us
  waiting for transfers between devices  392 us (49%)
  starting transfers between devices  165 us (21%)
  local copies, waits for them, and re-layouts  121 us (15%)
  Pallas kernels  101 us (13%)
  other arithmetic  13.1 us (2%)
    ppermute x19, waiting for transfers between devices, permute(): return lax.ppermute(values, ('row', 'col'), pairs)  392 us
    ppermute x19, starting transfers between devices, permute(): return lax.ppermute(values, ('row', 'col'), pairs)  165 us
    unnamed x10, local copies, waits for them, and re-layouts  57.9 us
    pallas_call x1, Pallas kernels, on_device(): pl.pallas_call(functools.partial(first_kernel, group, rows), grid=(ratio,...  51.5 us
    pallas_call x1, Pallas kernels, on_device(): pl.pallas_call(functools.partial(second_kernel, pieces, rows, tall), grid...  17.7 us
    pallas_call x1, Pallas kernels, on_device(): pl.pallas_call(functools.partial(last_kernel, quarters, ratio, rows, wind...  17.5 us
  transfers between devices with their start and end apart: 19, of which 10 were waited for; matrix products, arithmetic and copies ran while one was open for 6% of the time, Pallas kernels for 2%

profile of v1, /device:TPU:6, one launch (start us, length us, event | category | flops | bytes accessed | tf_op | source)
XLA Modules:
  0.0 793.3 jit_solution(17045221308122147164)
XLA Ops:
  0.0 54.5 %copy.29.d_ref = f32[2,40,32,20,160]{4,3,2,1,0:T(8,128)} copy(f32[2,40,32,20,160]{4,2,3,1,0:T(8,128)} %param.9) | data formatting | bytes 65536000 | tf_op args[0]
  54.5 0.7 tile.10.v_ref
  55.2 51.5 %first_dimension.1 = (f32[4,2,40,20,256]{4,3,2,1,0:T(8,128)}, f32[2,40,20,1024]{3,2,1,0:T(8,128)}) custom-call(f32[2,40,32,20,160]{4,3,2,1,0:T(8,128)} %copy.29.d_ref, f32[20,128]{1,0:T(8,128)} %tile.10.v_ref, bf16[32,160,256]{2,1,0:T(8,128)(2,1)} %constant.260.clone.high_ref, bf16[32,160,256]{2,1,0:T(8,128)(2,1)} %constant.261.clone.low_ref, ...), custom_call_target="tpu_custom_call" | custom-call | flops 20000000000 | bytes 80000000 | tf_op jit(solution)/shard_map/first_dimension/pallas_call | solution.py:177
  106.7 4.1 constant_dynamic-slice_fusion.11
  110.8 0.6 copy.96
  111.4 4.5 collective-permute-start
  115.9 0.6 copy.95
  116.5 1.3 collective-permute-start.1
  118.4 0.9 collective-permute-start.2
  119.3 1.5 copy.93
  120.8 2.7 collective-permute-start.3
  123.5 1.5 copy.92
  125.2 1.5 copy.91
  127.4 0.6 copy.89
  128.0 104.6 %collective-permute-done = f32[2,20,20,256]{3,0,2,1:T(2,128)S(1)} collective-permute-done((f32[2,20,20,256]{3,0,2,1:T(2,128)S(1)}, f32[2,20,20,256]{3,0,2,1:T(2,128)S(1)}, u32[]{:S(2)}, u32[]{:S(2)}) %collective-permute-start) | collective-permute-done | bytes 819232 | tf_op jit(solution)/shard_map/ppermute | solution.py:205
  232.7 26.3 %collective-permute-done.1 = f32[2,20,20,256]{3,0,2,1:T(2,128)S(1)} collective-permute-done((f32[2,20,20,256]{3,0,2,1:T(2,128)S(1)}, f32[2,20,20,256]{3,0,2,1:T(2,128)S(1)}, u32[]{:S(2)}, u32[]{:S(2)}) %collective-permute-start.1) | collective-permute-done | bytes 819232 | tf_op jit(solution)/shard_map/ppermute | solution.py:205
  259.0 20.7 %collective-permute-start.7 = (f32[2,20,20,256]{3,0,2,1:T(2,128)S(1)}, f32[2,20,20,256]{3,0,2,1:T(2,128)}, u32[]{:S(2)}, u32[]{:S(2)}) collective-permute-start(f32[2,20,20,256]{3,0,2,1:T(2,128)S(1)} %bitcast.121), channel_id=1, source_target_pairs={{0,7},{1,15},{2,23},{3,31},{4,3},{5,11},{6,19},{7,27},{8,4},{9,12}... | collective-permute-start | bytes 2457608 | tf_op jit(solution)/shard_map/ppermute | solution.py:205
  279.6 14.2 %mirror_first.1 = f32[4,2,2,20,20,256]{5,4,3,2,1,0:T(8,128)} custom-call(f32[2,40,20,1024]{3,2,1,0:T(8,128)} %get-tuple-element.8.l_ref, bf16[1024,1024]{1,0:T(8,128)(2,1)} %constant.263.clone.perm_ref), custom_call_target="tpu_custom_call" | custom-call | flops 20000000000 | bytes 16000000 | tf_op jit(solution)/shard_map/mirror_first/pallas_call | solution.py:224
  293.9 2.5 dynamic-slice_bitcast_fusion
  296.4 2.2 concatenate.6
  298.6 2.1 concatenate.7
  300.7 1.0 copy.38.refs_0_
  301.7 1.0 copy.39.refs_1_
  302.8 2.2 copy.40.refs_2_
  305.0 2.2 copy.41.refs_3_
  307.2 2.2 copy.42.refs_4_
  309.4 2.2 copy.43.refs_5_
  311.6 2.2 copy.44.refs_6_
  313.7 2.2 copy.45.refs_7_
  316.0 17.7 %second_dimension.1 = f32[8,2,20,20,256]{4,3,2,1,0:T(8,128)} custom-call(s32[1]{0:T(128)} %bitcast.3.start_ref, f32[2,20,20,256]{3,2,1,0:T(8,128)} %copy.38.refs_0_, f32[2,20,20,256]{3,2,1,0:T(8,128)} %copy.39.refs_1_, f32[2,20,20,256]{3,2,1,0:T(8,128)} %copy.40.refs_2_, f32[2,20,20,256]{3,2,1,0:T(8,128)} %copy.41.refs_3_, f32[2,20,20,256]{3,2,1,0:T(8,128)} %copy.42.refs_4_, ...), custom_call_target="tpu_custom_call" | custom-call | tf_op jit(solution)/shard_map/second_dimension/pallas_call | solution.py:255
  333.7 4.8 bitcast_add_fusion.3
  338.5 2.4 copy.46
  341.0 40.6 %collective-permute-start.8 = (f32[2,2,20,20,256]{4,1,3,2,0:T(2,128)}, f32[2,2,20,20,256]{4,1,3,2,0:T(2,128)}, u32[]{:S(2)}, u32[]{:S(2)}) collective-permute-start(f32[2,2,20,20,256]{4,1,3,2,0:T(2,128)} %copy.46), channel_id=1, source_target_pairs={{0,1},{1,2},{2,3},{3,0},{4,5},{5,6},{6,7},{7,4},{8,9},{9,10},{10,1... | collective-permute-start | bytes 4915208 | tf_op jit(solution)/shard_map/ppermute | solution.py:205
  381.6 2.4 copy.50
  384.0 48.1 %collective-permute-start.10 = (f32[2,2,20,20,256]{4,1,3,2,0:T(2,128)}, f32[2,2,20,20,256]{4,1,3,2,0:T(2,128)}, u32[]{:S(2)}, u32[]{:S(2)}) collective-permute-start(f32[2,2,20,20,256]{4,1,3,2,0:T(2,128)} %copy.50), channel_id=1, source_target_pairs={{0,3},{1,0},{2,1},{3,2},{4,7},{5,4},{6,5},{7,6},{8,11},{9,8},{10,9... | collective-permute-start | bytes 4915208 | tf_op jit(solution)/shard_map/ppermute | solution.py:205
  432.1 2.5 copy.48
  435.1 1.5 copy.88
  436.7 7.4 collective-permute-start.11
  445.4 4.0 collective-permute-start.12
  449.4 46.5 %collective-permute-done.11 = f32[2,20,20,256]{3,0,2,1:T(2,128)} collective-permute-done((f32[2,20,20,256]{3,0,2,1:T(2,128)}, f32[2,20,20,256]{3,0,2,1:T(2,128)}, u32[]{:S(2)}, u32[]{:S(2)}) %collective-permute-start.11) | collective-permute-done | bytes 819232 | tf_op jit(solution)/shard_map/ppermute | solution.py:205
  495.9 1.4 bitcast_dynamic-update-slice_fusion.7
  497.4 39.0 %collective-permute-done.9 = f32[2,2,20,20,256]{4,1,3,2,0:T(2,128)} collective-permute-done((f32[2,2,20,20,256]{4,1,3,2,0:T(2,128)}, f32[2,2,20,20,256]{4,1,3,2,0:T(2,128)}, u32[]{:S(2)}, u32[]{:S(2)}) %collective-permute-start.9) | collective-permute-done | bytes 1638432 | tf_op jit(solution)/shard_map/ppermute | solution.py:205
  536.4 4.9 bitcast_add_fusion.2
  541.5 0.6 copy.86
  542.1 7.8 collective-permute-start.13
  550.3 0.6 copy.85
  550.9 3.6 collective-permute-start.14
  554.7 0.6 copy.84
  555.3 1.9 collective-permute-start.15
  557.3 0.6 copy.83
  557.9 1.2 collective-permute-start.16
  559.3 0.6 copy.82
  559.9 6.0 collective-permute-start.17
  565.9 3.4 pad_maximum_fusion.y_ref
  569.9 89.1 %collective-permute-done.13 = f32[2,20,20,256]{3,0,2,1:T(2,128)S(1)} collective-permute-done((f32[2,20,20,256]{3,0,2,1:T(2,128)S(1)}, f32[2,20,20,256]{3,0,2,1:T(2,128)S(1)}, u32[]{:S(2)}, u32[]{:S(2)}) %collective-permute-start.13) | collective-permute-done | bytes 819232 | tf_op jit(solution)/shard_map/ppermute | solution.py:205
  659.0 13.9 %collective-permute-start.18 = (f32[2,20,20,256]{3,0,2,1:T(2,128)S(1)}, f32[2,20,20,256]{3,0,2,1:T(2,128)S(1)}, u32[]{:S(2)}, u32[]{:S(2)}) collective-permute-start(f32[2,20,20,256]{3,0,2,1:T(2,128)S(1)} %bitcast.130), channel_id=1, source_target_pairs={{0,4},{1,12},{2,20},{3,28},{4,0},{5,8},{6,16},{7,24},{8,5},{9,13},... | collective-permute-start | bytes 2457608 | tf_op jit(solution)/shard_map/ppermute | solution.py:205
  673.2 17.7 %collective-permute-done.14 = f32[2,20,20,256]{3,0,2,1:T(2,128)S(1)} collective-permute-done((f32[2,20,20,256]{3,0,2,1:T(2,128)S(1)}, f32[2,20,20,256]{3,0,2,1:T(2,128)S(1)}, u32[]{:S(2)}, u32[]{:S(2)}) %collective-permute-start.14) | collective-permute-done | bytes 819232 | tf_op jit(solution)/shard_map/ppermute | solution.py:205
  691.3 11.6 %collective-permute-done.15 = f32[2,20,20,256]{3,0,2,1:T(2,128)S(1)} collective-permute-done((f32[2,20,20,256]{3,0,2,1:T(2,128)S(1)}, f32[2,20,20,256]{3,0,2,1:T(2,128)S(1)}, u32[]{:S(2)}, u32[]{:S(2)}) %collective-permute-start.15) | collective-permute-done | bytes 819232 | tf_op jit(solution)/shard_map/ppermute | solution.py:205
  703.3 22.8 %collective-permute-done.16 = f32[2,20,20,256]{3,0,2,1:T(2,128)S(1)} collective-permute-done((f32[2,20,20,256]{3,0,2,1:T(2,128)S(1)}, f32[2,20,20,256]{3,0,2,1:T(2,128)S(1)}, u32[]{:S(2)}, u32[]{:S(2)}) %collective-permute-start.16) | collective-permute-done | bytes 819232 | tf_op jit(solution)/shard_map/ppermute | solution.py:205
  726.4 11.6 %collective-permute-done.17 = f32[2,20,20,256]{3,0,2,1:T(2,128)S(1)} collective-permute-done((f32[2,20,20,256]{3,0,2,1:T(2,128)S(1)}, f32[2,20,20,256]{3,0,2,1:T(2,128)S(1)}, u32[]{:S(2)}, u32[]{:S(2)}) %collective-permute-start.17) | collective-permute-done | bytes 819232 | tf_op jit(solution)/shard_map/ppermute | solution.py:205
  738.4 22.7 %collective-permute-done.18 = f32[2,20,20,256]{3,0,2,1:T(2,128)S(1)} collective-permute-done((f32[2,20,20,256]{3,0,2,1:T(2,128)S(1)}, f32[2,20,20,256]{3,0,2,1:T(2,128)S(1)}, u32[]{:S(2)}, u32[]{:S(2)}) %collective-permute-start.18) | collective-permute-done | bytes 819232 | tf_op jit(solution)/shard_map/ppermute | solution.py:205
  761.4 4.1 copy.60
  765.6 17.5 %combine.1 = f32[2,40,20,1024]{3,2,1,0:T(8,128)} custom-call(s32[5]{0:T(128)} %stack.65.where_ref, f32[4,2,2,20,20,256]{5,4,3,2,1,0:T(8,128)} %pad_maximum_fusion.y_ref, f32[4,2,2,20,20,256]{5,4,3,2,1,0:T(8,128)} %bitcast.116, f32[4,2,40,20,256]{4,3,2,1,0:T(8,128)} %get-tuple-element.7.w_ref, bf16[1024,1024]{1,0:T(8,128)(2,1)} %constant.263.clone.perm_ref, ...), custom_call_target="tpu_custom_call" | custom-call | tf_op jit(solution)/shard_map/combine/pallas_call | solution.py:285
  783.0 9.8 %copy.61 = f32[2,40,20,1024]{3,1,2,0:T(8,128)} copy(f32[2,40,20,1024]{3,2,1,0:T(8,128)} %combine.1) | data formatting | bytes 13107200 | tf_op jit(solution)/shard_map/combine/pallas_call | solution.py:285
  (34 shorter events, 6.7 us)
Async XLA Ops:
  0.0 54.5 %slice-start = ((f32[20,160]{1,0:T(8,128)}), f32[20,32]{1,0:T(8,128)S(1)}, s32[]{:S(2)}) async-start(f32[20,160]{1,0:T(8,128)} %param.10), calls=%async_computation | async-start | bytes 24576 | tf_op jit(solution)/shard_map/slice | solution.py:170
  111.4 121.3 %collective-permute-start = (f32[2,20,20,256]{3,0,2,1:T(2,128)S(1)}, f32[2,20,20,256]{3,0,2,1:T(2,128)S(1)}, u32[]{:S(2)}, u32[]{:S(2)}) collective-permute-start(f32[2,20,20,256]{3,0,2,1:T(2,128)S(1)} %bitcast.132), channel_id=1, source_target_pairs={{0,0},{1,8},{2,16},{3,24},{4,4},{5,12},{6,20},{7,28},{8,1},{9,9},{... | collective-permute-start | bytes 2457608 | tf_op jit(solution)/shard_map/ppermute | solution.py:205
  116.5 142.4 %collective-permute-start.1 = (f32[2,20,20,256]{3,0,2,1:T(2,128)S(1)}, f32[2,20,20,256]{3,0,2,1:T(2,128)S(1)}, u32[]{:S(2)}, u32[]{:S(2)}) collective-permute-start(f32[2,20,20,256]{3,0,2,1:T(2,128)S(1)} %bitcast.131), channel_id=1, source_target_pairs={{0,4},{1,12},{2,20},{3,28},{4,0},{5,8},{6,16},{7,24},{8,5},{9,13},... | collective-permute-start | bytes 2457608 | tf_op jit(solution)/shard_map/ppermute | solution.py:205
  118.4 140.5 %collective-permute-start.2 = (f32[2,20,20,256]{3,0,2,1:T(2,128)S(1)}, f32[2,20,20,256]{3,0,2,1:T(2,128)S(1)}, u32[]{:S(2)}, u32[]{:S(2)}) collective-permute-start(f32[2,20,20,256]{3,0,2,1:T(2,128)S(1)} %bitcast.129), channel_id=1, source_target_pairs={{0,1},{1,9},{2,17},{3,25},{4,5},{5,13},{6,21},{7,29},{8,2},{9,10},... | collective-permute-start | bytes 2457608 | tf_op jit(solution)/shard_map/ppermute | solution.py:205
  120.8 184.1 %collective-permute-start.3 = (f32[2,20,20,256]{3,0,2,1:T(2,128)}, f32[2,20,20,256]{3,0,2,1:T(2,128)}, u32[]{:S(2)}, u32[]{:S(2)}) collective-permute-start(f32[2,20,20,256]{3,0,2,1:T(2,128)} %bitcast.112), channel_id=1, source_target_pairs={{0,5},{1,13},{2,21},{3,29},{4,1},{5,9},{6,17},{7,25},{8,6},{9,14},... | collective-permute-start | bytes 2457608 | tf_op jit(solution)/shard_map/ppermute | solution.py:205
  125.1 182.1 %collective-permute-start.4 = (f32[2,20,20,256]{3,0,2,1:T(2,128)}, f32[2,20,20,256]{3,0,2,1:T(2,128)}, u32[]{:S(2)}, u32[]{:S(2)}) collective-permute-start(f32[2,20,20,256]{3,0,2,1:T(2,128)} %bitcast.111), channel_id=1, source_target_pairs={{0,2},{1,10},{2,18},{3,26},{4,6},{5,14},{6,22},{7,30},{8,3},{9,11}... | collective-permute-start | bytes 2457608 | tf_op jit(solution)/shard_map/ppermute | solution.py:205
  232.7 76.7 %collective-permute-start.5 = (f32[2,20,20,256]{3,0,2,1:T(2,128)}, f32[2,20,20,256]{3,0,2,1:T(2,128)}, u32[]{:S(2)}, u32[]{:S(2)}) collective-permute-start(f32[2,20,20,256]{3,0,2,1:T(2,128)} %bitcast.110), channel_id=1, source_target_pairs={{0,6},{1,14},{2,22},{3,30},{4,2},{5,10},{6,18},{7,26},{8,7},{9,15}... | collective-permute-start | bytes 2457608 | tf_op jit(solution)/shard_map/ppermute | solution.py:205
  258.9 52.6 %collective-permute-start.6 = (f32[2,20,20,256]{3,0,2,1:T(2,128)S(1)}, f32[2,20,20,256]{3,0,2,1:T(2,128)}, u32[]{:S(2)}, u32[]{:S(2)}) collective-permute-start(f32[2,20,20,256]{3,0,2,1:T(2,128)S(1)} %bitcast.122), channel_id=1, source_target_pairs={{0,3},{1,11},{2,19},{3,27},{4,7},{5,15},{6,23},{7,31},{8,0},{9,8},... | collective-permute-start | bytes 2457608 | tf_op jit(solution)/shard_map/ppermute | solution.py:205
  259.0 20.7 %copy-start = (f32[2,20,20,256]{3,0,2,1:T(2,128)}, f32[2,20,20,256]{3,0,2,1:T(2,128)S(1)}, u32[]{:S(2)}) copy-start(f32[2,20,20,256]{3,0,2,1:T(2,128)S(1)} %collective-permute-done.2) | copy-start | bytes 2457604
  259.0 54.8 %collective-permute-start.7 = (f32[2,20,20,256]{3,0,2,1:T(2,128)S(1)}, f32[2,20,20,256]{3,0,2,1:T(2,128)}, u32[]{:S(2)}, u32[]{:S(2)}) collective-permute-start(f32[2,20,20,256]{3,0,2,1:T(2,128)S(1)} %bitcast.121), channel_id=1, source_target_pairs={{0,7},{1,15},{2,23},{3,31},{4,3},{5,11},{6,19},{7,27},{8,4},{9,12}... | collective-permute-start | bytes 2457608 | tf_op jit(solution)/shard_map/ppermute | solution.py:205
  341.0 156.4 %collective-permute-start.8 = (f32[2,2,20,20,256]{4,1,3,2,0:T(2,128)}, f32[2,2,20,20,256]{4,1,3,2,0:T(2,128)}, u32[]{:S(2)}, u32[]{:S(2)}) collective-permute-start(f32[2,2,20,20,256]{4,1,3,2,0:T(2,128)} %copy.46), channel_id=1, source_target_pairs={{0,1},{1,2},{2,3},{3,0},{4,5},{5,6},{6,7},{7,4},{8,9},{9,10},{10,1... | collective-permute-start | bytes 4915208 | tf_op jit(solution)/shard_map/ppermute | solution.py:205
  384.0 113.3 %collective-permute-start.10 = (f32[2,2,20,20,256]{4,1,3,2,0:T(2,128)}, f32[2,2,20,20,256]{4,1,3,2,0:T(2,128)}, u32[]{:S(2)}, u32[]{:S(2)}) collective-permute-start(f32[2,2,20,20,256]{4,1,3,2,0:T(2,128)} %copy.50), channel_id=1, source_target_pairs={{0,3},{1,0},{2,1},{3,2},{4,7},{5,4},{6,5},{7,6},{8,11},{9,8},{10,9... | collective-permute-start | bytes 4915208 | tf_op jit(solution)/shard_map/ppermute | solution.py:205
  434.6 101.8 %collective-permute-start.9 = (f32[2,2,20,20,256]{4,1,3,2,0:T(2,128)}, f32[2,2,20,20,256]{4,1,3,2,0:T(2,128)}, u32[]{:S(2)}, u32[]{:S(2)}) collective-permute-start(f32[2,2,20,20,256]{4,1,3,2,0:T(2,128)} %copy.48), channel_id=1, source_target_pairs={{0,2},{1,3},{2,0},{3,1},{4,6},{5,7},{6,4},{7,5},{8,10},{9,11},{10,... | collective-permute-start | bytes 4915208 | tf_op jit(solution)/shard_map/ppermute | solution.py:205
  436.7 59.2 %collective-permute-start.11 = (f32[2,20,20,256]{3,0,2,1:T(2,128)}, f32[2,20,20,256]{3,0,2,1:T(2,128)}, u32[]{:S(2)}, u32[]{:S(2)}) collective-permute-start(f32[2,20,20,256]{3,0,2,1:T(2,128)} %bitcast.107), channel_id=1, source_target_pairs={{0,0},{1,8},{2,16},{3,24},{4,4},{5,12},{6,20},{7,28},{8,1},{9,9},{... | collective-permute-start | bytes 2457608 | tf_op jit(solution)/shard_map/ppermute | solution.py:205
  445.4 104.6 %collective-permute-start.12 = (f32[2,20,20,256]{3,0,2,1:T(2,128)S(1)}, f32[2,20,20,256]{3,0,2,1:T(2,128)S(1)}, u32[]{:S(2)}, u32[]{:S(2)}) collective-permute-start(f32[2,20,20,256]{3,0,2,1:T(2,128)S(1)} %bitcast.128), channel_id=1, source_target_pairs={{0,4},{1,12},{2,20},{3,28},{4,0},{5,8},{6,16},{7,24},{8,5},{9,13},... | collective-permute-start | bytes 2457608 | tf_op jit(solution)/shard_map/ppermute | solution.py:205
  542.1 116.9 %collective-permute-start.13 = (f32[2,20,20,256]{3,0,2,1:T(2,128)S(1)}, f32[2,20,20,256]{3,0,2,1:T(2,128)S(1)}, u32[]{:S(2)}, u32[]{:S(2)}) collective-permute-start(f32[2,20,20,256]{3,0,2,1:T(2,128)S(1)} %bitcast.123), channel_id=1, source_target_pairs={{0,0},{1,8},{2,16},{3,24},{4,4},{5,12},{6,20},{7,28},{8,1},{9,9},{... | collective-permute-start | bytes 2457608 | tf_op jit(solution)/shard_map/ppermute | solution.py:205
  550.9 140.0 %collective-permute-start.14 = (f32[2,20,20,256]{3,0,2,1:T(2,128)S(1)}, f32[2,20,20,256]{3,0,2,1:T(2,128)S(1)}, u32[]{:S(2)}, u32[]{:S(2)}) collective-permute-start(f32[2,20,20,256]{3,0,2,1:T(2,128)S(1)} %bitcast.124), channel_id=1, source_target_pairs={{0,4},{1,12},{2,20},{3,28},{4,0},{5,8},{6,16},{7,24},{8,5},{9,13},... | collective-permute-start | bytes 2457608 | tf_op jit(solution)/shard_map/ppermute | solution.py:205
  555.3 147.6 %collective-permute-start.15 = (f32[2,20,20,256]{3,0,2,1:T(2,128)S(1)}, f32[2,20,20,256]{3,0,2,1:T(2,128)S(1)}, u32[]{:S(2)}, u32[]{:S(2)}) collective-permute-start(f32[2,20,20,256]{3,0,2,1:T(2,128)S(1)} %bitcast.125), channel_id=1, source_target_pairs={{0,0},{1,8},{2,16},{3,24},{4,4},{5,12},{6,20},{7,28},{8,1},{9,9},{... | collective-permute-start | bytes 2457608 | tf_op jit(solution)/shard_map/ppermute | solution.py:205
  557.9 168.2 %collective-permute-start.16 = (f32[2,20,20,256]{3,0,2,1:T(2,128)S(1)}, f32[2,20,20,256]{3,0,2,1:T(2,128)S(1)}, u32[]{:S(2)}, u32[]{:S(2)}) collective-permute-start(f32[2,20,20,256]{3,0,2,1:T(2,128)S(1)} %bitcast.126), channel_id=1, source_target_pairs={{0,4},{1,12},{2,20},{3,28},{4,0},{5,8},{6,16},{7,24},{8,5},{9,13},... | collective-permute-start | bytes 2457608 | tf_op jit(solution)/shard_map/ppermute | solution.py:205
  559.9 178.1 %collective-permute-start.17 = (f32[2,20,20,256]{3,0,2,1:T(2,128)S(1)}, f32[2,20,20,256]{3,0,2,1:T(2,128)S(1)}, u32[]{:S(2)}, u32[]{:S(2)}) collective-permute-start(f32[2,20,20,256]{3,0,2,1:T(2,128)S(1)} %bitcast.127), channel_id=1, source_target_pairs={{0,0},{1,8},{2,16},{3,24},{4,4},{5,12},{6,20},{7,28},{8,1},{9,9},{... | collective-permute-start | bytes 2457608 | tf_op jit(solution)/shard_map/ppermute | solution.py:205
  659.0 102.1 %collective-permute-start.18 = (f32[2,20,20,256]{3,0,2,1:T(2,128)S(1)}, f32[2,20,20,256]{3,0,2,1:T(2,128)S(1)}, u32[]{:S(2)}, u32[]{:S(2)}) collective-permute-start(f32[2,20,20,256]{3,0,2,1:T(2,128)S(1)} %bitcast.130), channel_id=1, source_target_pairs={{0,4},{1,12},{2,20},{3,28},{4,0},{5,8},{6,16},{7,24},{8,5},{9,13},... | collective-permute-start | bytes 2457608 | tf_op jit(solution)/shard_map/ppermute | solution.py:205

commit v2 on v1

--- a/solution.py
+++ b/solution.py
@@ -44,7 +44,7 @@
     return (n + 7) // 8 * 8
 
 
-def first_kernel(group, rows, d_ref, v_ref, high_ref, low_ref, eye_ref, w_ref, l_ref, pad):
+def first_kernel(group, rows, d_ref, v_ref, high_ref, low_ref, eye_ref, l_ref, pad):
     blocks, tall = pad.shape[0], pad.shape[1]
 
     @pl.when((pl.program_id(0) == 0) & (pl.program_id(1) == 0))
@@ -63,8 +63,6 @@
         window.append(win.reshape(blocks, tall, LANES)[:, :rows])
         mixed.append(mix.reshape(blocks, tall, 2 * LANES)[:, :rows])
     v = v_ref[...][None]
-    w_ref[0, 0] = window[0]
-    w_ref[0, 1] = window[1]
     l_ref[0] = mixed[1][..., :LANES] + mixed[0][..., LANES:] + v * window[1]
     l_ref[1] = mixed[1][..., LANES:] - mixed[0][..., :LANES] - v * window[0]
 
@@ -165,16 +163,19 @@
         weights[q, :, LANES + at : LANES + at + window] = -friction * (e - q)[None, :] * slope[:window].T
         if q < group:
             eyes[q, e, at + e] = 1.0
+    taken = jnp.transpose(density[..., :window], (0, 1, 3, 2, 4))
+    per = window // quarters
+    w_all = jnp.stack(
+        [
+            taken[:, :, :, u * per : (u + 1) * per].reshape(2, cols, rows, wide)
+            for u in range(quarters)
+        ]
+    )
     whigh, wlow = split_host(weights)
     eye = jnp.asarray(eyes.astype(jnp.bfloat16))
     tiled = jnp.tile(potential[:, :window], (1, group))
 
-    per = max(1, LANES // wide)
-    unit = min(wide, LANES)
-    store = max(wide, LANES)
-    stores = lanes // store
-    inner = store // LANES
-    w_all, l_all = pl.pallas_call(
+    l_all, = pl.pallas_call(
         functools.partial(first_kernel, group, rows),
         grid=(ratio, groups),
         in_specs=[
@@ -185,11 +186,9 @@
             pl.BlockSpec((group, width, LANES), lambda h, m: (0, 0, 0)),
         ],
         out_specs=[
-            pl.BlockSpec((1, 2, rows, rows, LANES), lambda h, m: (m // inner, 0, h, 0, m % inner)),
             pl.BlockSpec((2, rows, rows, LANES), lambda h, m: (0, h, 0, m)),
         ],
         out_shape=[
-            jax.ShapeDtypeStruct((stores, 2, cols, rows, store), f32),
             jax.ShapeDtypeStruct((2, cols, rows, lanes), f32),
         ],
         scratch_shapes=[pltpu.VMEM((rows, tall, width), f32)],
@@ -197,9 +196,6 @@
         cost_estimate=pl.CostEstimate(flops=2 * 10**10, bytes_accessed=80 * 10**6, transcendentals=0),
         name="first_dimension",
     )(density, tiled, whigh, wlow, eye)
-    if per > 1:
-        w_all = jnp.moveaxis(w_all.reshape(stores, 2, cols, rows, per, wide), 4, 1).reshape(quarters, 2, cols, rows, wide)
-
     def permute(values, target):
         pairs = [(r * n_col + c, target(r, c)) for r in range(n_row) for c in range(n_col)]
         return lax.ppermute(values, ("row", "col"), pairs)

time: 803 us -> 761 us (0.948)
  waiting for transfers between devices: 392 us -> 283 us
  local copies, waits for them, and re-layouts: 121 us -> 189 us
    ppermute x19, waiting for transfers between devices: 392 us -> 283 us  [permute(): return lax.ppermute(values, ('row', 'col'), pairs)]
    another operation x0 -> x5, local copies, waits for them, and re-layouts: none -> 21.4 us  [on_device(): jnp.stack([taken[:, :, :, u * per:(u + 1) * per].reshape(2, cols, rows, w...]
    transpose x0 -> x1, local copies, waits for them, and re-layouts: none -> 19.5 us  [on_device(): taken = jnp.transpose(density[..., :window], (0, 1, 3, 2, 4))]
    slice x0 -> x1, local copies, waits for them, and re-layouts: none -> 18.2 us  [on_device(): taken[:, :, :, u * per:(u + 1) * per].reshape(2, cols, rows, wide)]
    unnamed x10 -> x13, local copies, waits for them, and re-layouts: 57.9 us -> 63.8 us
  transfers between devices with their start and end apart: 19 -> 19, of which waited for: 10 -> 11; matrix products, arithmetic and copies ran while one was open for 6% -> 14% of each run, Pallas kernels for 2% -> 9%
where the time goes in v2:
time: 761 us; the launch traced here: 751 us
  waiting for transfers between devices  283 us (37%)
  local copies, waits for them, and re-layouts  189 us (25%)
  starting transfers between devices  166 us (22%)
  Pallas kernels  100 us (13%)
  other arithmetic  13.1 us (2%)
    ppermute x19, waiting for transfers between devices, permute(): return lax.ppermute(values, ('row', 'col'), pairs)  283 us
    ppermute x19, starting transfers between devices, permute(): return lax.ppermute(values, ('row', 'col'), pairs)  166 us
    unnamed x13, local copies, waits for them, and re-layouts  63.8 us
    pallas_call x1, Pallas kernels, on_device(): pl.pallas_call(functools.partial(first_kernel, group, rows), grid=(ratio,...  50.8 us
    another operation x5, local copies, waits for them, and re-layouts, on_device(): jnp.stack([taken[:, :, :, u * per:(u + 1) * per].reshape(2, cols, rows, w...  21.4 us
    transpose x1, local copies, waits for them, and re-layouts, on_device(): taken = jnp.transpose(density[..., :window], (0, 1, 3, 2, 4))  19.5 us
    slice x1, local copies, waits for them, and re-layouts, on_device(): taken[:, :, :, u * per:(u + 1) * per].reshape(2, cols, rows, wide)  18.2 us
    pallas_call x1, Pallas kernels, on_device(): pl.pallas_call(functools.partial(second_kernel, pieces, rows, tall), grid...  17.7 us
  transfers between devices with their start and end apart: 19, of which 11 were waited for; matrix products, arithmetic and copies ran while one was open for 14% of the time, Pallas kernels for 9%

profile of v2, /device:TPU:6, one launch (start us, length us, event | category | flops | bytes accessed | tf_op | source)
XLA Modules:
  0.0 751.3 jit_solution(5625401829664889950)
XLA Ops:
  0.0 19.5 %slice_bitcast_fusion = f32[2,40,20,32,32]{4,3,2,1,0:T(8,128)} fusion(f32[2,40,32,20,160]{4,2,3,1,0:T(8,128)} %param.9), kind=kLoop, calls=%fused_computation | loop fusion | bytes 13107200 | tf_op jit(solution)/shard_map/transpose | solution.py:166
  19.5 18.2 %fusion = (f32[2,40,20,8,32]{4,3,2,1,0:T(8,128)}, f32[2,40,20,8,32]{4,3,2,1,0:T(8,128)}, f32[2,40,20,8,32]{4,3,2,1,0:T(8,128)}, f32[2,40,20,8,32]{4,3,2,1,0:T(8,128)}) fusion(f32[2,40,20,32,32]{4,3,2,1,0:T(8,128)} %slice_bitcast_fusion), kind=kLoop, calls=%fused_computation.69 | loop fusion | bytes 13107200 | tf_op jit(solution)/shard_map/slice | solution.py:170
  37.7 4.4 reshape.9
  43.6 4.4 reshape.10
  48.1 5.6 reshape.11
  53.6 5.5 reshape.12
  60.6 3.0 constant_dynamic-update-slice_fusion.1
  63.6 1.4 constant_dynamic-update-slice_fusion.w_ref
  65.0 4.1 constant_dynamic-slice_fusion.11
  69.1 1.5 copy.126
  70.6 4.5 collective-permute-start
  75.1 1.6 copy.125
  77.9 1.5 copy.124
  80.2 1.5 copy.123
  81.8 2.7 collective-permute-start.3
  84.4 1.5 copy.122
  86.0 4.0 collective-permute-start.4
  89.9 54.5 %copy.71.d_ref = f32[2,40,32,20,160]{4,3,2,1,0:T(8,128)} copy(f32[2,40,32,20,160]{4,2,3,1,0:T(8,128)} %param.9) | data formatting | bytes 65536000 | tf_op args[0]
  145.1 50.8 %first_dimension.1.l_ref = f32[2,40,20,1024]{3,2,1,0:T(8,128)} custom-call(f32[2,40,32,20,160]{4,3,2,1,0:T(8,128)} %copy.71.d_ref, f32[20,128]{1,0:T(8,128)} %tile.10.v_ref, bf16[32,160,256]{2,1,0:T(8,128)(2,1)} %constant.260.clone.high_ref, bf16[32,160,256]{2,1,0:T(8,128)(2,1)} %constant.261.clone.low_ref, bf16[4,160,128]{2,1,0:T(8,128)(2,1)} %constant.262.clone.eye_ref), custom_call_target="tpu_custom_call" | custom-call | flops 20000000000 | bytes 80000000 | tf_op jit(solution)/shard_map/first_dimension/pallas_call | solution.py:178
  195.9 1.5 copy.121
  199.0 2.0 collective-permute-done.1
  200.9 3.3 collective-permute-start.7
  204.2 14.2 %mirror_first.1 = f32[4,2,2,20,20,256]{5,4,3,2,1,0:T(8,128)} custom-call(f32[2,40,20,1024]{3,2,1,0:T(8,128)} %first_dimension.1.l_ref, bf16[1024,1024]{1,0:T(8,128)(2,1)} %constant.263.clone.perm_ref), custom_call_target="tpu_custom_call" | custom-call | flops 20000000000 | bytes 16000000 | tf_op jit(solution)/shard_map/mirror_first/pallas_call | solution.py:220
  218.5 2.3 dynamic-slice_bitcast_fusion
  220.8 2.2 concatenate.6
  223.9 2.2 copy.63.refs_0_
  226.1 2.2 copy.64.refs_1_
  228.3 2.2 copy.65.refs_2_
  230.5 2.2 copy.66.refs_3_
  232.7 2.2 copy.67.refs_4_
  235.9 2.6 collective-permute-done.6
  238.5 2.2 copy.69.refs_6_
  240.7 7.5 %collective-permute-done.7 = f32[2,20,20,256]{3,0,2,1:T(2,128)} collective-permute-done((f32[2,20,20,256]{3,0,2,1:T(2,128)S(1)}, f32[2,20,20,256]{3,0,2,1:T(2,128)}, u32[]{:S(2)}, u32[]{:S(2)}) %collective-permute-start.7) | collective-permute-done | bytes 819232 | tf_op jit(solution)/shard_map/ppermute | solution.py:201
  248.2 2.2 copy.70.refs_7_
  250.4 17.7 %second_dimension.1 = f32[8,2,20,20,256]{4,3,2,1,0:T(8,128)} custom-call(s32[1]{0:T(128)} %bitcast.3.start_ref, f32[2,20,20,256]{3,2,1,0:T(8,128)} %copy.63.refs_0_, f32[2,20,20,256]{3,2,1,0:T(8,128)} %copy.64.refs_1_, f32[2,20,20,256]{3,2,1,0:T(8,128)} %copy.65.refs_2_, f32[2,20,20,256]{3,2,1,0:T(8,128)} %copy.66.refs_3_, f32[2,20,20,256]{3,2,1,0:T(8,128)} %copy.67.refs_4_, ...), custom_call_target="tpu_custom_call" | custom-call | tf_op jit(solution)/shard_map/second_dimension/pallas_call | solution.py:251
  268.1 4.8 bitcast_add_fusion.3
  273.0 2.4 copy.72
  275.4 54.1 %collective-permute-start.8 = (f32[2,2,20,20,256]{4,1,3,2,0:T(2,128)}, f32[2,2,20,20,256]{4,1,3,2,0:T(2,128)}, u32[]{:S(2)}, u32[]{:S(2)}) collective-permute-start(f32[2,2,20,20,256]{4,1,3,2,0:T(2,128)} %copy.72), channel_id=1, source_target_pairs={{0,1},{1,2},{2,3},{3,0},{4,5},{5,6},{6,7},{7,4},{8,9},{9,10},{10,1... | collective-permute-start | bytes 4915208 | tf_op jit(solution)/shard_map/ppermute | solution.py:201
  329.5 2.4 copy.76
  332.0 62.4 %collective-permute-start.10 = (f32[2,2,20,20,256]{4,1,3,2,0:T(2,128)}, f32[2,2,20,20,256]{4,1,3,2,0:T(2,128)}, u32[]{:S(2)}, u32[]{:S(2)}) collective-permute-start(f32[2,2,20,20,256]{4,1,3,2,0:T(2,128)} %copy.76), channel_id=1, source_target_pairs={{0,3},{1,0},{2,1},{3,2},{4,7},{5,4},{6,5},{7,6},{8,11},{9,8},{10,9... | collective-permute-start | bytes 4915208 | tf_op jit(solution)/shard_map/ppermute | solution.py:201
  394.4 2.5 copy.74
  397.4 1.5 copy.118
  398.9 3.0 collective-permute-start.11
  403.2 4.0 collective-permute-start.12
  407.2 51.1 %collective-permute-done.11 = f32[2,20,20,256]{3,0,2,1:T(2,128)} collective-permute-done((f32[2,20,20,256]{3,0,2,1:T(2,128)}, f32[2,20,20,256]{3,0,2,1:T(2,128)}, u32[]{:S(2)}, u32[]{:S(2)}) %collective-permute-start.11) | collective-permute-done | bytes 819232 | tf_op jit(solution)/shard_map/ppermute | solution.py:201
  458.2 1.4 bitcast_dynamic-update-slice_fusion.7
  459.7 39.1 %collective-permute-done.9 = f32[2,2,20,20,256]{4,1,3,2,0:T(2,128)} collective-permute-done((f32[2,2,20,20,256]{4,1,3,2,0:T(2,128)}, f32[2,2,20,20,256]{4,1,3,2,0:T(2,128)}, u32[]{:S(2)}, u32[]{:S(2)}) %collective-permute-start.9) | collective-permute-done | bytes 1638432 | tf_op jit(solution)/shard_map/ppermute | solution.py:201
  498.8 4.9 bitcast_add_fusion.2
  504.6 3.1 collective-permute-start.13
  508.7 3.6 collective-permute-start.14
  513.1 2.2 collective-permute-start.15
  515.9 3.6 collective-permute-start.16
  520.3 3.4 collective-permute-start.17
  523.7 3.4 pad_maximum_fusion.y_ref
  527.8 93.9 %collective-permute-done.13 = f32[2,20,20,256]{3,0,2,1:T(2,128)S(1)} collective-permute-done((f32[2,20,20,256]{3,0,2,1:T(2,128)S(1)}, f32[2,20,20,256]{3,0,2,1:T(2,128)S(1)}, u32[]{:S(2)}, u32[]{:S(2)}) %collective-permute-start.13) | collective-permute-done | bytes 819232 | tf_op jit(solution)/shard_map/ppermute | solution.py:201
  621.6 9.2 %collective-permute-start.18 = (f32[2,20,20,256]{3,0,2,1:T(2,128)S(1)}, f32[2,20,20,256]{3,0,2,1:T(2,128)S(1)}, u32[]{:S(2)}, u32[]{:S(2)}) collective-permute-start(f32[2,20,20,256]{3,0,2,1:T(2,128)S(1)} %bitcast.139), channel_id=1, source_target_pairs={{0,4},{1,12},{2,20},{3,28},{4,0},{5,8},{6,16},{7,24},{8,5},{9,13},... | collective-permute-start | bytes 2457608 | tf_op jit(solution)/shard_map/ppermute | solution.py:201
  631.2 17.7 %collective-permute-done.14 = f32[2,20,20,256]{3,0,2,1:T(2,128)S(1)} collective-permute-done((f32[2,20,20,256]{3,0,2,1:T(2,128)S(1)}, f32[2,20,20,256]{3,0,2,1:T(2,128)S(1)}, u32[]{:S(2)}, u32[]{:S(2)}) %collective-permute-start.14) | collective-permute-done | bytes 819232 | tf_op jit(solution)/shard_map/ppermute | solution.py:201
  649.3 16.3 %collective-permute-done.15 = f32[2,20,20,256]{3,0,2,1:T(2,128)S(1)} collective-permute-done((f32[2,20,20,256]{3,0,2,1:T(2,128)S(1)}, f32[2,20,20,256]{3,0,2,1:T(2,128)S(1)}, u32[]{:S(2)}, u32[]{:S(2)}) %collective-permute-start.15) | collective-permute-done | bytes 819232 | tf_op jit(solution)/shard_map/ppermute | solution.py:201
  665.9 18.2 %collective-permute-done.16 = f32[2,20,20,256]{3,0,2,1:T(2,128)S(1)} collective-permute-done((f32[2,20,20,256]{3,0,2,1:T(2,128)S(1)}, f32[2,20,20,256]{3,0,2,1:T(2,128)S(1)}, u32[]{:S(2)}, u32[]{:S(2)}) %collective-permute-start.16) | collective-permute-done | bytes 819232 | tf_op jit(solution)/shard_map/ppermute | solution.py:201
  684.4 16.3 %collective-permute-done.17 = f32[2,20,20,256]{3,0,2,1:T(2,128)S(1)} collective-permute-done((f32[2,20,20,256]{3,0,2,1:T(2,128)S(1)}, f32[2,20,20,256]{3,0,2,1:T(2,128)S(1)}, u32[]{:S(2)}, u32[]{:S(2)}) %collective-permute-start.17) | collective-permute-done | bytes 819232 | tf_op jit(solution)/shard_map/ppermute | solution.py:201
  701.0 18.1 %collective-permute-done.18 = f32[2,20,20,256]{3,0,2,1:T(2,128)S(1)} collective-permute-done((f32[2,20,20,256]{3,0,2,1:T(2,128)S(1)}, f32[2,20,20,256]{3,0,2,1:T(2,128)S(1)}, u32[]{:S(2)}, u32[]{:S(2)}) %collective-permute-start.18) | collective-permute-done | bytes 819232 | tf_op jit(solution)/shard_map/ppermute | solution.py:201
  719.4 4.1 copy.86
  723.5 17.5 %combine.1 = f32[2,40,20,1024]{3,2,1,0:T(8,128)} custom-call(s32[5]{0:T(128)} %stack.68.where_ref, f32[4,2,2,20,20,256]{5,4,3,2,1,0:T(8,128)} %pad_maximum_fusion.y_ref, f32[4,2,2,20,20,256]{5,4,3,2,1,0:T(8,128)} %bitcast.126, f32[4,2,40,20,256]{4,3,2,1,0:T(8,128)} %constant_dynamic-update-slice_fusion.w_ref, bf16[1024,1024]{1,0:T(8,128)(2,1)} %constant.263.clone.perm_ref, ...), custom_call_target="tpu_custom_call" | custom-call | tf_op jit(solution)/shard_map/combine/pallas_call | solution.py:281
  741.0 9.8 %copy.87 = f32[2,40,20,1024]{3,1,2,0:T(8,128)} copy(f32[2,40,20,1024]{3,2,1,0:T(8,128)} %combine.1) | data formatting | bytes 13107200 | tf_op jit(solution)/shard_map/combine/pallas_call | solution.py:281
  (44 shorter events, 17.5 us)
Async XLA Ops:
  59.2 4.4 copy-start
  70.6 128.1 %collective-permute-start = (f32[2,20,20,256]{3,0,2,1:T(2,128)}, f32[2,20,20,256]{3,0,2,1:T(2,128)}, u32[]{:S(2)}, u32[]{:S(2)}) collective-permute-start(f32[2,20,20,256]{3,0,2,1:T(2,128)} %bitcast.125), channel_id=1, source_target_pairs={{0,0},{1,8},{2,16},{3,24},{4,4},{5,12},{6,20},{7,28},{8,1},{9,9},{... | collective-permute-start | bytes 2457608 | tf_op jit(solution)/shard_map/ppermute | solution.py:201
  76.7 124.3 %collective-permute-start.1 = (f32[2,20,20,256]{3,0,2,1:T(2,128)}, f32[2,20,20,256]{3,0,2,1:T(2,128)}, u32[]{:S(2)}, u32[]{:S(2)}) collective-permute-start(f32[2,20,20,256]{3,0,2,1:T(2,128)} %bitcast.124), channel_id=1, source_target_pairs={{0,4},{1,12},{2,20},{3,28},{4,0},{5,8},{6,16},{7,24},{8,5},{9,13},... | collective-permute-start | bytes 2457608 | tf_op jit(solution)/shard_map/ppermute | solution.py:201
  79.4 121.5 %collective-permute-start.2 = (f32[2,20,20,256]{3,0,2,1:T(2,128)}, f32[2,20,20,256]{3,0,2,1:T(2,128)}, u32[]{:S(2)}, u32[]{:S(2)}) collective-permute-start(f32[2,20,20,256]{3,0,2,1:T(2,128)} %bitcast.123), channel_id=1, source_target_pairs={{0,1},{1,9},{2,17},{3,25},{4,5},{5,13},{6,21},{7,29},{8,2},{9,10},... | collective-permute-start | bytes 2457608 | tf_op jit(solution)/shard_map/ppermute | solution.py:201
  81.8 148.7 %collective-permute-start.3 = (f32[2,20,20,256]{3,0,2,1:T(2,128)}, f32[2,20,20,256]{3,0,2,1:T(2,128)}, u32[]{:S(2)}, u32[]{:S(2)}) collective-permute-start(f32[2,20,20,256]{3,0,2,1:T(2,128)} %bitcast.122), channel_id=1, source_target_pairs={{0,5},{1,13},{2,21},{3,29},{4,1},{5,9},{6,17},{7,25},{8,6},{9,14},... | collective-permute-start | bytes 2457608 | tf_op jit(solution)/shard_map/ppermute | solution.py:201
  86.0 58.5 %slice-start = ((f32[20,160]{1,0:T(8,128)}), f32[20,32]{1,0:T(8,128)S(1)}, s32[]{:S(2)}) async-start(f32[20,160]{1,0:T(8,128)} %param.10), calls=%async_computation | async-start | bytes 24576 | tf_op jit(solution)/shard_map/slice | solution.py:176
  86.0 146.7 %collective-permute-start.4 = (f32[2,20,20,256]{3,0,2,1:T(2,128)}, f32[2,20,20,256]{3,0,2,1:T(2,128)}, u32[]{:S(2)}, u32[]{:S(2)}) collective-permute-start(f32[2,20,20,256]{3,0,2,1:T(2,128)} %bitcast.121), channel_id=1, source_target_pairs={{0,2},{1,10},{2,18},{3,26},{4,6},{5,14},{6,22},{7,30},{8,3},{9,11}... | collective-permute-start | bytes 2457608 | tf_op jit(solution)/shard_map/ppermute | solution.py:201
  198.8 36.1 %collective-permute-start.5 = (f32[2,20,20,256]{3,0,2,1:T(2,128)}, f32[2,20,20,256]{3,0,2,1:T(2,128)S(1)}, u32[]{:S(2)}, u32[]{:S(2)}) collective-permute-start(f32[2,20,20,256]{3,0,2,1:T(2,128)} %bitcast.120), channel_id=1, source_target_pairs={{0,6},{1,14},{2,22},{3,30},{4,2},{5,10},{6,18},{7,26},{8,7},{9,15}... | collective-permute-start | bytes 2457608 | tf_op jit(solution)/shard_map/ppermute | solution.py:201
  200.9 37.6 %collective-permute-start.6 = (f32[2,20,20,256]{3,0,2,1:T(2,128)S(1)}, f32[2,20,20,256]{3,0,2,1:T(2,128)}, u32[]{:S(2)}, u32[]{:S(2)}) collective-permute-start(f32[2,20,20,256]{3,0,2,1:T(2,128)S(1)} %bitcast.132), channel_id=1, source_target_pairs={{0,3},{1,11},{2,19},{3,27},{4,7},{5,15},{6,23},{7,31},{8,0},{9,8},... | collective-permute-start | bytes 2457608 | tf_op jit(solution)/shard_map/ppermute | solution.py:201
  200.9 47.3 %collective-permute-start.7 = (f32[2,20,20,256]{3,0,2,1:T(2,128)S(1)}, f32[2,20,20,256]{3,0,2,1:T(2,128)}, u32[]{:S(2)}, u32[]{:S(2)}) collective-permute-start(f32[2,20,20,256]{3,0,2,1:T(2,128)S(1)} %bitcast.131), channel_id=1, source_target_pairs={{0,7},{1,15},{2,23},{3,31},{4,3},{5,11},{6,19},{7,27},{8,4},{9,12}... | collective-permute-start | bytes 2457608 | tf_op jit(solution)/shard_map/ppermute | solution.py:201
  275.4 184.3 %collective-permute-start.8 = (f32[2,2,20,20,256]{4,1,3,2,0:T(2,128)}, f32[2,2,20,20,256]{4,1,3,2,0:T(2,128)}, u32[]{:S(2)}, u32[]{:S(2)}) collective-permute-start(f32[2,2,20,20,256]{4,1,3,2,0:T(2,128)} %copy.72), channel_id=1, source_target_pairs={{0,1},{1,2},{2,3},{3,0},{4,5},{5,6},{6,7},{7,4},{8,9},{9,10},{10,1... | collective-permute-start | bytes 4915208 | tf_op jit(solution)/shard_map/ppermute | solution.py:201
  332.0 127.7 %collective-permute-start.10 = (f32[2,2,20,20,256]{4,1,3,2,0:T(2,128)}, f32[2,2,20,20,256]{4,1,3,2,0:T(2,128)}, u32[]{:S(2)}, u32[]{:S(2)}) collective-permute-start(f32[2,2,20,20,256]{4,1,3,2,0:T(2,128)} %copy.76), channel_id=1, source_target_pairs={{0,3},{1,0},{2,1},{3,2},{4,7},{5,4},{6,5},{7,6},{8,11},{9,8},{10,9... | collective-permute-start | bytes 4915208 | tf_op jit(solution)/shard_map/ppermute | solution.py:201
  396.8 102.0 %collective-permute-start.9 = (f32[2,2,20,20,256]{4,1,3,2,0:T(2,128)}, f32[2,2,20,20,256]{4,1,3,2,0:T(2,128)}, u32[]{:S(2)}, u32[]{:S(2)}) collective-permute-start(f32[2,2,20,20,256]{4,1,3,2,0:T(2,128)} %copy.74), channel_id=1, source_target_pairs={{0,2},{1,3},{2,0},{3,1},{4,6},{5,7},{6,4},{7,5},{8,10},{9,11},{10,... | collective-permute-start | bytes 4915208 | tf_op jit(solution)/shard_map/ppermute | solution.py:201
  398.9 59.3 %collective-permute-start.11 = (f32[2,20,20,256]{3,0,2,1:T(2,128)}, f32[2,20,20,256]{3,0,2,1:T(2,128)}, u32[]{:S(2)}, u32[]{:S(2)}) collective-permute-start(f32[2,20,20,256]{3,0,2,1:T(2,128)} %bitcast.117), channel_id=1, source_target_pairs={{0,0},{1,8},{2,16},{3,24},{4,4},{5,12},{6,20},{7,28},{8,1},{9,9},{... | collective-permute-start | bytes 2457608 | tf_op jit(solution)/shard_map/ppermute | solution.py:201
  403.2 104.5 %collective-permute-start.12 = (f32[2,20,20,256]{3,0,2,1:T(2,128)S(1)}, f32[2,20,20,256]{3,0,2,1:T(2,128)S(1)}, u32[]{:S(2)}, u32[]{:S(2)}) collective-permute-start(f32[2,20,20,256]{3,0,2,1:T(2,128)S(1)} %bitcast.138), channel_id=1, source_target_pairs={{0,4},{1,12},{2,20},{3,28},{4,0},{5,8},{6,16},{7,24},{8,5},{9,13},... | collective-permute-start | bytes 2457608 | tf_op jit(solution)/shard_map/ppermute | solution.py:201
  504.6 117.1 %collective-permute-start.13 = (f32[2,20,20,256]{3,0,2,1:T(2,128)S(1)}, f32[2,20,20,256]{3,0,2,1:T(2,128)S(1)}, u32[]{:S(2)}, u32[]{:S(2)}) collective-permute-start(f32[2,20,20,256]{3,0,2,1:T(2,128)S(1)} %bitcast.133), channel_id=1, source_target_pairs={{0,0},{1,8},{2,16},{3,24},{4,4},{5,12},{6,20},{7,28},{8,1},{9,9},{... | collective-permute-start | bytes 2457608 | tf_op jit(solution)/shard_map/ppermute | solution.py:201
  508.7 140.2 %collective-permute-start.14 = (f32[2,20,20,256]{3,0,2,1:T(2,128)S(1)}, f32[2,20,20,256]{3,0,2,1:T(2,128)S(1)}, u32[]{:S(2)}, u32[]{:S(2)}) collective-permute-start(f32[2,20,20,256]{3,0,2,1:T(2,128)S(1)} %bitcast.134), channel_id=1, source_target_pairs={{0,4},{1,12},{2,20},{3,28},{4,0},{5,8},{6,16},{7,24},{8,5},{9,13},... | collective-permute-start | bytes 2457608 | tf_op jit(solution)/shard_map/ppermute | solution.py:201
  513.1 152.4 %collective-permute-start.15 = (f32[2,20,20,256]{3,0,2,1:T(2,128)S(1)}, f32[2,20,20,256]{3,0,2,1:T(2,128)S(1)}, u32[]{:S(2)}, u32[]{:S(2)}) collective-permute-start(f32[2,20,20,256]{3,0,2,1:T(2,128)S(1)} %bitcast.135), channel_id=1, source_target_pairs={{0,0},{1,8},{2,16},{3,24},{4,4},{5,12},{6,20},{7,28},{8,1},{9,9},{... | collective-permute-start | bytes 2457608 | tf_op jit(solution)/shard_map/ppermute | solution.py:201
  515.9 168.1 %collective-permute-start.16 = (f32[2,20,20,256]{3,0,2,1:T(2,128)S(1)}, f32[2,20,20,256]{3,0,2,1:T(2,128)S(1)}, u32[]{:S(2)}, u32[]{:S(2)}) collective-permute-start(f32[2,20,20,256]{3,0,2,1:T(2,128)S(1)} %bitcast.136), channel_id=1, source_target_pairs={{0,4},{1,12},{2,20},{3,28},{4,0},{5,8},{6,16},{7,24},{8,5},{9,13},... | collective-permute-start | bytes 2457608 | tf_op jit(solution)/shard_map/ppermute | solution.py:201
  520.3 180.3 %collective-permute-start.17 = (f32[2,20,20,256]{3,0,2,1:T(2,128)S(1)}, f32[2,20,20,256]{3,0,2,1:T(2,128)S(1)}, u32[]{:S(2)}, u32[]{:S(2)}) collective-permute-start(f32[2,20,20,256]{3,0,2,1:T(2,128)S(1)} %bitcast.137), channel_id=1, source_target_pairs={{0,0},{1,8},{2,16},{3,24},{4,4},{5,12},{6,20},{7,28},{8,1},{9,9},{... | collective-permute-start | bytes 2457608 | tf_op jit(solution)/shard_map/ppermute | solution.py:201
  621.6 97.4 %collective-permute-start.18 = (f32[2,20,20,256]{3,0,2,1:T(2,128)S(1)}, f32[2,20,20,256]{3,0,2,1:T(2,128)S(1)}, u32[]{:S(2)}, u32[]{:S(2)}) collective-permute-start(f32[2,20,20,256]{3,0,2,1:T(2,128)S(1)} %bitcast.139), channel_id=1, source_target_pairs={{0,4},{1,12},{2,20},{3,28},{4,0},{5,8},{6,16},{7,24},{8,5},{9,13},... | collective-permute-start | bytes 2457608 | tf_op jit(solution)/shard_map/ppermute | solution.py:201

commit v3 on v2

--- a/solution.py
+++ b/solution.py
@@ -200,6 +200,23 @@
         pairs = [(r * n_col + c, target(r, c)) for r in range(n_row) for c in range(n_col)]
         return lax.ppermute(values, ("row", "col"), pairs)
 
+    def swap(values, target, early):
+        half = n_col // 2
+        direct, first, last = [], [], []
+        for r in range(n_row):
+            for c in range(n_col):
+                to_r, to_c = target(r, c)
+                here, there = r * n_col + c, to_r * n_col + to_c
+                if c // half == to_c // half:
+                    direct.append((here, there))
+                    continue
+                via = r * n_col + (c + half) % n_col if early else to_r * n_col + (to_c + half) % n_col
+                first.append((here, via))
+                last.append((via, there))
+        axes = ("row", "col")
+        moved = lax.ppermute(lax.ppermute(values, axes, first), axes, last)
+        return moved + lax.ppermute(values, axes, direct)
+
     def to_middle(j, k):
         return lambda r, c: (c * ratio + (r % ratio + j) % ratio) * n_col + (r // ratio + k) % n_col
 
@@ -271,7 +288,7 @@
         for j in range(ratio):
             out = lax.dynamic_index_in_dim(half, (own + j) % ratio, 0, keepdims=False)
             arrived.append(
-                permute(out, lambda r, c, j=j: (c * ratio + (r % ratio + j) % ratio) * n_col + r // ratio)
+                swap(out, lambda r, c, j=j: (c * ratio + (r % ratio + j) % ratio, r // ratio), j % 2 == 0)
             )
     mine = jnp.stack(mine)
     arrived = jnp.stack(arrived).reshape(n_col, ratio, 2, rows, rows, wide)

time: 761 us -> 698 us (0.917)
  the two profiles are of different devices: /device:TPU:6 before, /device:TPU:19 now
where the time goes in v3:
time: 698 us; the launch traced here: 688 us
  waiting for transfers between devices  250 us (36%)
  local copies, waits for them, and re-layouts  189 us (27%)
  starting transfers between devices  125 us (18%)
  Pallas kernels  100 us (14%)
  other arithmetic  22.5 us (3%)
    ppermute x16, waiting for transfers between devices, swap(): moved = lax.ppermute(lax.ppermute(values, axes, first), axes, last)  141 us
    ppermute x11, waiting for transfers between devices, permute(): return lax.ppermute(values, ('row', 'col'), pairs)  88 us
    unnamed x44, local copies, waits for them, and re-layouts  61.4 us
    ppermute x11, starting transfers between devices, permute(): return lax.ppermute(values, ('row', 'col'), pairs)  54.9 us
    pallas_call x1, Pallas kernels, on_device(): pl.pallas_call(functools.partial(first_kernel, group, rows), grid=(ratio,...  50.8 us
    ppermute x16, starting transfers between devices, swap(): moved = lax.ppermute(lax.ppermute(values, axes, first), axes, last)  43.4 us
    ppermute x8, starting transfers between devices, swap(): return moved + lax.ppermute(values, axes, direct)  27 us
    another operation x5, local copies, waits for them, and re-layouts, on_device(): jnp.stack([taken[:, :, :, u * per:(u + 1) * per].reshape(2, cols, rows, w...  21.4 us
  transfers between devices with their start and end apart: 35, of which 11 were waited for; matrix products, arithmetic and copies ran while one was open for 17% of the time, Pallas kernels for 9%

profile of v3, /device:TPU:19, one launch (start us, length us, event | category | flops | bytes accessed | tf_op | source)
XLA Modules:
  0.0 688.3 jit_solution(10032278648716852679)
XLA Ops:
  0.0 19.4 %slice_bitcast_fusion = f32[2,40,20,32,32]{4,3,2,1,0:T(8,128)} fusion(f32[2,40,32,20,160]{4,2,3,1,0:T(8,128)} %param.9), kind=kLoop, calls=%fused_computation | loop fusion | bytes 13107200 | tf_op jit(solution)/shard_map/transpose | solution.py:166
  19.4 18.3 %fusion = (f32[2,40,20,8,32]{4,3,2,1,0:T(8,128)}, f32[2,40,20,8,32]{4,3,2,1,0:T(8,128)}, f32[2,40,20,8,32]{4,3,2,1,0:T(8,128)}, f32[2,40,20,8,32]{4,3,2,1,0:T(8,128)}) fusion(f32[2,40,20,32,32]{4,3,2,1,0:T(8,128)} %slice_bitcast_fusion), kind=kLoop, calls=%fused_computation.69 | loop fusion | bytes 13107200 | tf_op jit(solution)/shard_map/slice | solution.py:170
  37.7 4.4 reshape.9
  43.6 4.4 reshape.10
  48.0 5.6 reshape.11
  53.6 5.6 reshape.12
  60.6 3.0 constant_dynamic-update-slice_fusion.1
  65.0 4.1 constant_dynamic-slice_fusion.11
  70.6 3.8 collective-permute-start
  76.9 1.6 copy.124
  78.4 5.7 collective-permute-start.2
  84.1 1.6 copy.123
  85.7 1.5 copy.122
  88.4 54.6 %copy.71.d_ref = f32[2,40,32,20,160]{4,3,2,1,0:T(8,128)} copy(f32[2,40,32,20,160]{4,2,3,1,0:T(8,128)} %param.9) | data formatting | bytes 65536000 | tf_op args[0]
  143.7 50.8 %first_dimension.1.l_ref = f32[2,40,20,1024]{3,2,1,0:T(8,128)} custom-call(f32[2,40,32,20,160]{4,3,2,1,0:T(8,128)} %copy.71.d_ref, f32[20,128]{1,0:T(8,128)} %tile.10.v_ref, bf16[32,160,256]{2,1,0:T(8,128)(2,1)} %constant.260.clone.high_ref, bf16[32,160,256]{2,1,0:T(8,128)(2,1)} %constant.261.clone.low_ref, bf16[4,160,128]{2,1,0:T(8,128)(2,1)} %constant.262.clone.eye_ref), custom_call_target="tpu_custom_call" | custom-call | flops 20000000000 | bytes 80000000 | tf_op jit(solution)/shard_map/first_dimension/pallas_call | solution.py:178
  198.8 3.3 collective-permute-start.6
  203.3 14.3 %mirror_first.1 = f32[4,2,2,20,20,256]{5,4,3,2,1,0:T(8,128)} custom-call(f32[2,40,20,1024]{3,2,1,0:T(8,128)} %first_dimension.1.l_ref, bf16[1024,1024]{1,0:T(8,128)(2,1)} %constant.263.clone.perm_ref), custom_call_target="tpu_custom_call" | custom-call | flops 20000000000 | bytes 16000000 | tf_op jit(solution)/shard_map/mirror_first/pallas_call | solution.py:237
  217.6 2.3 dynamic-slice_bitcast_fusion
  219.9 2.2 concatenate.6
  223.1 2.2 copy.63.refs_0_
  225.3 2.2 copy.64.refs_1_
  227.5 2.2 copy.65.refs_2_
  229.7 2.2 copy.66.refs_3_
  231.9 71.7 %collective-permute-done.4 = f32[2,20,20,256]{3,0,2,1:T(2,128)} collective-permute-done((f32[2,20,20,256]{3,0,2,1:T(2,128)}, f32[2,20,20,256]{3,0,2,1:T(2,128)}, u32[]{:S(2)}, u32[]{:S(2)}) %collective-permute-start.4) | collective-permute-done | bytes 819232 | tf_op jit(solution)/shard_map/ppermute | solution.py:201
  303.6 2.2 copy.67.refs_4_
  305.8 16.2 %collective-permute-done.5 = f32[2,20,20,256]{3,0,2,1:T(2,128)S(1)} collective-permute-done((f32[2,20,20,256]{3,0,2,1:T(2,128)}, f32[2,20,20,256]{3,0,2,1:T(2,128)S(1)}, u32[]{:S(2)}, u32[]{:S(2)}) %collective-permute-start.5) | collective-permute-done | bytes 819232 | tf_op jit(solution)/shard_map/ppermute | solution.py:201
  323.1 2.2 copy.69.refs_6_
  325.3 2.2 copy.70.refs_7_
  327.5 17.7 %second_dimension.1 = f32[8,2,20,20,256]{4,3,2,1,0:T(8,128)} custom-call(s32[1]{0:T(128)} %bitcast.3.start_ref, f32[2,20,20,256]{3,2,1,0:T(8,128)} %copy.63.refs_0_, f32[2,20,20,256]{3,2,1,0:T(8,128)} %copy.64.refs_1_, f32[2,20,20,256]{3,2,1,0:T(8,128)} %copy.65.refs_2_, f32[2,20,20,256]{3,2,1,0:T(8,128)} %copy.66.refs_3_, f32[2,20,20,256]{3,2,1,0:T(8,128)} %copy.67.refs_4_, ...), custom_call_target="tpu_custom_call" | custom-call | tf_op jit(solution)/shard_map/second_dimension/pallas_call | solution.py:268
  345.2 4.8 bitcast_add_fusion.3
  350.0 2.4 copy.72
  352.5 37.2 %collective-permute-start.8 = (f32[2,2,20,20,256]{4,1,3,2,0:T(2,128)}, f32[2,2,20,20,256]{4,1,3,2,0:T(2,128)}, u32[]{:S(2)}, u32[]{:S(2)}) collective-permute-start(f32[2,2,20,20,256]{4,1,3,2,0:T(2,128)} %copy.72), channel_id=1, source_target_pairs={{0,1},{1,2},{2,3},{3,0},{4,5},{5,6},{6,7},{7,4},{8,9},{9,10},{10,1... | collective-permute-start | bytes 4915208 | tf_op jit(solution)/shard_map/ppermute | solution.py:201
  389.6 2.4 copy.76
  392.1 2.5 copy.74
  399.6 73.6 %collective-permute-done.11 = f32[2,20,20,256]{3,0,2,1:T(2,128)} collective-permute-done((f32[2,20,20,256]{3,0,2,1:T(2,128)}, f32[2,20,20,256]{3,0,2,1:T(2,128)}, u32[]{:S(2)}, u32[]{:S(2)}) %collective-permute-start.11) | collective-permute-done | bytes 819232 | tf_op jit(solution)/shard_map/ppermute | solution.py:217
  473.1 1.9 collective-permute-start.13
  475.0 4.7 collective-permute-start.16
  482.6 6.2 bitcast_add_fusion.2
  490.9 2.5 collective-permute-done.13
  493.4 4.2 collective-permute-start.19
  499.2 11.6 %collective-permute-done.16 = f32[2,20,20,256]{3,0,2,1:T(2,128)S(1)} collective-permute-done((f32[2,20,20,256]{3,0,2,1:T(2,128)S(1)}, f32[2,20,20,256]{3,0,2,1:T(2,128)S(1)}, u32[]{:S(2)}, u32[]{:S(2)}) %collective-permute-start.16) | collective-permute-done | bytes 819232 | tf_op jit(solution)/shard_map/ppermute | solution.py:218
  512.2 5.3 collective-permute-start.22
  519.7 2.1 collective-permute-start.25
  525.4 36.6 %collective-permute-done.20 = f32[2,20,20,256]{3,0,2,1:T(2,128)S(1)} collective-permute-done((f32[2,20,20,256]{3,0,2,1:T(2,128)}, f32[2,20,20,256]{3,0,2,1:T(2,128)S(1)}, u32[]{:S(2)}, u32[]{:S(2)}) %collective-permute-start.20) | collective-permute-done | bytes 819232 | tf_op jit(solution)/shard_map/ppermute | solution.py:217
  562.9 1.9 collective-permute-start.28
  565.4 1.8 constant_dynamic-slice_fusion.10
  568.5 2.3 collective-permute-start.18
  570.9 4.2 pad_maximum_fusion.y_ref
  576.5 4.1 collective-permute-start.21
  581.1 8.6 %collective-permute-done.26 = f32[2,20,20,256]{3,0,2,1:T(2,128)} collective-permute-done((f32[2,20,20,256]{3,0,2,1:T(2,128)}, f32[2,20,20,256]{3,0,2,1:T(2,128)}, u32[]{:S(2)}, u32[]{:S(2)}) %collective-permute-start.26) | collective-permute-done | bytes 819232 | tf_op jit(solution)/shard_map/ppermute | solution.py:217
  591.0 13.3 %collective-permute-start.24 = (f32[2,20,20,256]{3,0,2,1:T(2,128)}, f32[2,20,20,256]{3,0,2,1:T(2,128)S(1)}, u32[]{:S(2)}, u32[]{:S(2)}) collective-permute-start(f32[2,20,20,256]{3,0,2,1:T(2,128)} %collective-permute-done.23), channel_id=1, source_target_pairs={{0,16},{1,24},{4,20},{5,28},{8,17},{9,25},{12,21},{13,29},{18,2},{... | collective-permute-start | bytes 2457608 | tf_op jit(solution)/shard_map/ppermute | solution.py:217
  604.8 11.0 %collective-permute-done.18 = f32[2,20,20,256]{3,0,2,1:T(2,128)S(1)} collective-permute-done((f32[2,20,20,256]{3,0,2,1:T(2,128)S(1)}, f32[2,20,20,256]{3,0,2,1:T(2,128)S(1)}, u32[]{:S(2)}, u32[]{:S(2)}) %collective-permute-start.18) | collective-permute-done | bytes 819232 | tf_op jit(solution)/shard_map/ppermute | solution.py:217
  615.8 7.4 %collective-permute-start.27 = (f32[2,20,20,256]{3,0,2,1:T(2,128)}, f32[2,20,20,256]{3,0,2,1:T(2,128)S(1)}, u32[]{:S(2)}, u32[]{:S(2)}) collective-permute-start(f32[2,20,20,256]{3,0,2,1:T(2,128)} %collective-permute-done.26), channel_id=1, source_target_pairs={{22,20},{30,28},{18,16},{26,24},{23,21},{31,29},{19,17},{27,25},{4... | collective-permute-start | bytes 2457608 | tf_op jit(solution)/shard_map/ppermute | solution.py:217
  623.7 1.9 collective-permute-start.31
  627.0 1.6 bitcast_dynamic-update-slice_fusion.4
  628.6 4.9 collective-permute-start.34
  633.6 1.8 collective-permute-start.33
  635.4 1.6 bitcast_dynamic-update-slice_fusion.3
  637.0 1.6 bitcast_dynamic-update-slice_fusion.2
  638.7 11.0 %collective-permute-done.30 = f32[2,20,20,256]{3,0,2,1:T(2,128)S(1)} collective-permute-done((f32[2,20,20,256]{3,0,2,1:T(2,128)S(1)}, f32[2,20,20,256]{3,0,2,1:T(2,128)S(1)}, u32[]{:S(2)}, u32[]{:S(2)}) %collective-permute-start.30) | collective-permute-done | bytes 819232 | tf_op jit(solution)/shard_map/ppermute | solution.py:217
  650.1 6.1 collective-permute-done.34
  656.7 4.1 copy.86
  660.8 17.5 %combine.1 = f32[2,40,20,1024]{3,2,1,0:T(8,128)} custom-call(s32[5]{0:T(128)} %stack.68.where_ref, f32[4,2,2,20,20,256]{5,4,3,2,1,0:T(8,128)} %pad_maximum_fusion.y_ref, f32[4,2,2,20,20,256]{5,4,3,2,1,0:T(8,128)} %bitcast.126, f32[4,2,40,20,256]{4,3,2,1,0:T(8,128)} %constant_dynamic-update-slice_fusion.w_ref, bf16[1024,1024]{1,0:T(8,128)(2,1)} %constant.263.clone.perm_ref, ...), custom_call_target="tpu_custom_call" | custom-call | tf_op jit(solution)/shard_map/combine/pallas_call | solution.py:298
  678.3 9.8 %copy.87 = f32[2,40,20,1024]{3,1,2,0:T(8,128)} copy(f32[2,40,20,1024]{3,2,1,0:T(8,128)} %combine.1) | data formatting | bytes 13107200 | tf_op jit(solution)/shard_map/combine/pallas_call | solution.py:298
  (114 shorter events, 45.3 us)
Async XLA Ops:
  59.2 4.4 copy-start.5
  70.6 126.8 %collective-permute-start = (f32[2,20,20,256]{3,0,2,1:T(2,128)}, f32[2,20,20,256]{3,0,2,1:T(2,128)}, u32[]{:S(2)}, u32[]{:S(2)}) collective-permute-start(f32[2,20,20,256]{3,0,2,1:T(2,128)} %bitcast.125), channel_id=1, source_target_pairs={{0,0},{1,8},{2,16},{3,24},{4,4},{5,12},{6,20},{7,28},{8,1},{9,9},{... | collective-permute-start | bytes 2457608 | tf_op jit(solution)/shard_map/ppermute | solution.py:201
  75.9 122.9 %collective-permute-start.1 = (f32[2,20,20,256]{3,0,2,1:T(2,128)}, f32[2,20,20,256]{3,0,2,1:T(2,128)}, u32[]{:S(2)}, u32[]{:S(2)}) collective-permute-start(f32[2,20,20,256]{3,0,2,1:T(2,128)} %bitcast.124), channel_id=1, source_target_pairs={{0,4},{1,12},{2,20},{3,28},{4,0},{5,8},{6,16},{7,24},{8,5},{9,13},... | collective-permute-start | bytes 2457608 | tf_op jit(solution)/shard_map/ppermute | solution.py:201
  78.4 123.6 %collective-permute-start.2 = (f32[2,20,20,256]{3,0,2,1:T(2,128)}, f32[2,20,20,256]{3,0,2,1:T(2,128)}, u32[]{:S(2)}, u32[]{:S(2)}) collective-permute-start(f32[2,20,20,256]{3,0,2,1:T(2,128)} %bitcast.123), channel_id=1, source_target_pairs={{0,1},{1,9},{2,17},{3,25},{4,5},{5,13},{6,21},{7,29},{8,2},{9,10},... | collective-permute-start | bytes 2457608 | tf_op jit(solution)/shard_map/ppermute | solution.py:201
  85.7 144.0 %collective-permute-start.3 = (f32[2,20,20,256]{3,0,2,1:T(2,128)}, f32[2,20,20,256]{3,0,2,1:T(2,128)}, u32[]{:S(2)}, u32[]{:S(2)}) collective-permute-start(f32[2,20,20,256]{3,0,2,1:T(2,128)} %bitcast.122), channel_id=1, source_target_pairs={{0,5},{1,13},{2,21},{3,29},{4,1},{5,9},{6,17},{7,25},{8,6},{9,14},... | collective-permute-start | bytes 2457608 | tf_op jit(solution)/shard_map/ppermute | solution.py:201
  87.2 55.8 %slice-start = ((f32[20,160]{1,0:T(8,128)}), f32[20,32]{1,0:T(8,128)S(1)}, s32[]{:S(2)}) async-start(f32[20,160]{1,0:T(8,128)} %param.10), calls=%async_computation | async-start | bytes 24576 | tf_op jit(solution)/shard_map/slice | solution.py:176
  87.2 216.4 %collective-permute-start.4 = (f32[2,20,20,256]{3,0,2,1:T(2,128)}, f32[2,20,20,256]{3,0,2,1:T(2,128)}, u32[]{:S(2)}, u32[]{:S(2)}) collective-permute-start(f32[2,20,20,256]{3,0,2,1:T(2,128)} %bitcast.121), channel_id=1, source_target_pairs={{0,2},{1,10},{2,18},{3,26},{4,6},{5,14},{6,22},{7,30},{8,3},{9,11}... | collective-permute-start | bytes 2457608 | tf_op jit(solution)/shard_map/ppermute | solution.py:201
  197.3 124.7 %collective-permute-start.5 = (f32[2,20,20,256]{3,0,2,1:T(2,128)}, f32[2,20,20,256]{3,0,2,1:T(2,128)S(1)}, u32[]{:S(2)}, u32[]{:S(2)}) collective-permute-start(f32[2,20,20,256]{3,0,2,1:T(2,128)} %bitcast.120), channel_id=1, source_target_pairs={{0,6},{1,14},{2,22},{3,30},{4,2},{5,10},{6,18},{7,26},{8,7},{9,15}... | collective-permute-start | bytes 2457608 | tf_op jit(solution)/shard_map/ppermute | solution.py:201
  198.8 124.3 %collective-permute-start.6 = (f32[2,20,20,256]{3,0,2,1:T(2,128)S(1)}, f32[2,20,20,256]{3,0,2,1:T(2,128)}, u32[]{:S(2)}, u32[]{:S(2)}) collective-permute-start(f32[2,20,20,256]{3,0,2,1:T(2,128)S(1)} %bitcast.132), channel_id=1, source_target_pairs={{0,3},{1,11},{2,19},{3,27},{4,7},{5,15},{6,23},{7,31},{8,0},{9,8},... | collective-permute-start | bytes 2457608 | tf_op jit(solution)/shard_map/ppermute | solution.py:201
  202.0 123.3 %collective-permute-start.7 = (f32[2,20,20,256]{3,0,2,1:T(2,128)S(1)}, f32[2,20,20,256]{3,0,2,1:T(2,128)}, u32[]{:S(2)}, u32[]{:S(2)}) collective-permute-start(f32[2,20,20,256]{3,0,2,1:T(2,128)S(1)} %bitcast.131), channel_id=1, source_target_pairs={{0,7},{1,15},{2,23},{3,31},{4,3},{5,11},{6,19},{7,27},{8,4},{9,12}... | collective-permute-start | bytes 2457608 | tf_op jit(solution)/shard_map/ppermute | solution.py:201
  350.0 44.7 %copy-start.3 = (f32[2,2,20,20,256]{4,3,2,1,0:T(8,128)}, f32[2,2,20,20,256]{4,3,2,1,0:T(8,128)S(1)}, u32[]{:S(2)}) copy-start(f32[2,2,20,20,256]{4,3,2,1,0:T(8,128)S(1)} %get-tuple-element.9) | copy-start | bytes 4915204
  352.5 127.3 %collective-permute-start.8 = (f32[2,2,20,20,256]{4,1,3,2,0:T(2,128)}, f32[2,2,20,20,256]{4,1,3,2,0:T(2,128)}, u32[]{:S(2)}, u32[]{:S(2)}) collective-permute-start(f32[2,2,20,20,256]{4,1,3,2,0:T(2,128)} %copy.72), channel_id=1, source_target_pairs={{0,1},{1,2},{2,3},{3,0},{4,5},{5,6},{6,7},{7,4},{8,9},{9,10},{10,1... | collective-permute-start | bytes 4915208 | tf_op jit(solution)/shard_map/ppermute | solution.py:201
  392.1 89.0 %collective-permute-start.10 = (f32[2,2,20,20,256]{4,1,3,2,0:T(2,128)}, f32[2,2,20,20,256]{4,1,3,2,0:T(2,128)}, u32[]{:S(2)}, u32[]{:S(2)}) collective-permute-start(f32[2,2,20,20,256]{4,1,3,2,0:T(2,128)} %copy.76), channel_id=1, source_target_pairs={{0,3},{1,0},{2,1},{3,2},{4,7},{5,4},{6,5},{7,6},{8,11},{9,8},{10,9... | collective-permute-start | bytes 4915208 | tf_op jit(solution)/shard_map/ppermute | solution.py:201
  394.5 88.1 %collective-permute-start.9 = (f32[2,2,20,20,256]{4,1,3,2,0:T(2,128)}, f32[2,2,20,20,256]{4,1,3,2,0:T(2,128)}, u32[]{:S(2)}, u32[]{:S(2)}) collective-permute-start(f32[2,2,20,20,256]{4,1,3,2,0:T(2,128)} %copy.74), channel_id=1, source_target_pairs={{0,2},{1,3},{2,0},{3,1},{4,6},{5,7},{6,4},{7,5},{8,10},{9,11},{10,... | collective-permute-start | bytes 4915208 | tf_op jit(solution)/shard_map/ppermute | solution.py:201
  396.3 76.8 %collective-permute-start.11 = (f32[2,20,20,256]{3,0,2,1:T(2,128)}, f32[2,20,20,256]{3,0,2,1:T(2,128)}, u32[]{:S(2)}, u32[]{:S(2)}) collective-permute-start(f32[2,20,20,256]{3,0,2,1:T(2,128)} %bitcast.117), channel_id=1, source_target_pairs={{2,0},{3,1},{6,4},{7,5},{10,8},{11,9},{14,12},{15,13},{16,18},{17,... | collective-permute-start | bytes 2457608 | tf_op jit(solution)/shard_map/ppermute | solution.py:217
  398.2 76.8 %collective-permute-start.14 = (f32[2,20,20,256]{3,0,2,1:T(2,128)S(1)}, f32[2,20,20,256]{3,0,2,1:T(2,128)}, u32[]{:S(2)}, u32[]{:S(2)}) collective-permute-start(f32[2,20,20,256]{3,0,2,1:T(2,128)S(1)} %bitcast.137), channel_id=1, source_target_pairs={{2,22},{3,30},{6,18},{7,26},{10,23},{11,31},{14,19},{15,27},{16,4}... | collective-permute-start | bytes 2457608 | tf_op jit(solution)/shard_map/ppermute | solution.py:217
  473.1 20.3 %collective-permute-start.13 = (f32[2,20,20,256]{3,0,2,1:T(2,128)}, f32[2,20,20,256]{3,0,2,1:T(2,128)S(1)}, u32[]{:S(2)}, u32[]{:S(2)}) collective-permute-start(f32[2,20,20,256]{3,0,2,1:T(2,128)} %bitcast.117), channel_id=1, source_target_pairs={{0,0},{1,8},{4,4},{5,12},{8,1},{9,9},{12,5},{13,13},{18,18},{19,26... | collective-permute-start | bytes 2457608 | tf_op jit(solution)/shard_map/ppermute | solution.py:218
  475.0 35.8 %collective-permute-start.16 = (f32[2,20,20,256]{3,0,2,1:T(2,128)S(1)}, f32[2,20,20,256]{3,0,2,1:T(2,128)S(1)}, u32[]{:S(2)}, u32[]{:S(2)}) collective-permute-start(f32[2,20,20,256]{3,0,2,1:T(2,128)S(1)} %bitcast.138), channel_id=1, source_target_pairs={{0,4},{1,12},{4,0},{5,8},{8,5},{9,13},{12,1},{13,9},{18,22},{19,30... | collective-permute-start | bytes 2457608 | tf_op jit(solution)/shard_map/ppermute | solution.py:218
  479.7 32.4 %collective-permute-start.12 = (f32[2,20,20,256]{3,0,2,1:T(2,128)}, f32[2,20,20,256]{3,0,2,1:T(2,128)S(1)}, u32[]{:S(2)}, u32[]{:S(2)}) collective-permute-start(f32[2,20,20,256]{3,0,2,1:T(2,128)} %collective-permute-done.11), channel_id=1, source_target_pairs={{0,16},{1,24},{4,20},{5,28},{8,17},{9,25},{12,21},{13,29},{18,2},{... | collective-permute-start | bytes 2457608 | tf_op jit(solution)/shard_map/ppermute | solution.py:217
  481.1 37.2 %collective-permute-start.15 = (f32[2,20,20,256]{3,0,2,1:T(2,128)}, f32[2,20,20,256]{3,0,2,1:T(2,128)S(1)}, u32[]{:S(2)}, u32[]{:S(2)}) collective-permute-start(f32[2,20,20,256]{3,0,2,1:T(2,128)} %collective-permute-done.14), channel_id=1, source_target_pairs={{22,20},{30,28},{18,16},{26,24},{23,21},{31,29},{19,17},{27,25},{4... | collective-permute-start | bytes 2457608 | tf_op jit(solution)/shard_map/ppermute | solution.py:217
  488.8 29.5 %copy-start.1 = (f32[2,2,20,20,256]{4,3,2,1,0:T(8,128)}, f32[2,2,20,20,256]{4,3,2,1,0:T(8,128)S(1)}, u32[]{:S(2)}) copy-start(f32[2,2,20,20,256]{4,3,2,1,0:T(8,128)S(1)} %get-tuple-element.15) | copy-start | bytes 4915204
  489.6 30.0 %collective-permute-start.17 = (f32[2,20,20,256]{3,0,2,1:T(2,128)S(1)}, f32[2,20,20,256]{3,0,2,1:T(2,128)S(1)}, u32[]{:S(2)}, u32[]{:S(2)}) collective-permute-start(f32[2,20,20,256]{3,0,2,1:T(2,128)S(1)} %bitcast.141), channel_id=1, source_target_pairs={{2,0},{3,1},{6,4},{7,5},{10,8},{11,9},{14,12},{15,13},{16,18},{17,... | collective-permute-start | bytes 2457608 | tf_op jit(solution)/shard_map/ppermute | solution.py:217
  493.4 30.7 %copy-start.8 = (f32[2,20,20,256]{3,0,2,1:T(2,128)}, f32[2,20,20,256]{3,0,2,1:T(2,128)S(1)}, u32[]{:S(2)}) copy-start(f32[2,20,20,256]{3,0,2,1:T(2,128)S(1)} %collective-permute-done.13) | copy-start | bytes 2457604
  493.4 30.7 %collective-permute-start.19 = (f32[2,20,20,256]{3,0,2,1:T(2,128)S(1)}, f32[2,20,20,256]{3,0,2,1:T(2,128)S(1)}, u32[]{:S(2)}, u32[]{:S(2)}) collective-permute-start(f32[2,20,20,256]{3,0,2,1:T(2,128)S(1)} %bitcast.142), channel_id=1, source_target_pairs={{0,0},{1,8},{4,4},{5,12},{8,1},{9,9},{12,5},{13,13},{18,18},{19,26... | collective-permute-start | bytes 2457608 | tf_op jit(solution)/shard_map/ppermute | solution.py:218
  510.8 13.2 %copy-start.6 = (f32[2,20,20,256]{3,0,2,1:T(2,128)}, f32[2,20,20,256]{3,0,2,1:T(2,128)S(1)}, u32[]{:S(2)}) copy-start(f32[2,20,20,256]{3,0,2,1:T(2,128)S(1)} %collective-permute-done.16) | copy-start | bytes 2457604
  510.8 51.1 %collective-permute-start.20 = (f32[2,20,20,256]{3,0,2,1:T(2,128)}, f32[2,20,20,256]{3,0,2,1:T(2,128)S(1)}, u32[]{:S(2)}, u32[]{:S(2)}) collective-permute-start(f32[2,20,20,256]{3,0,2,1:T(2,128)} %bitcast.114), channel_id=1, source_target_pairs={{2,22},{3,30},{6,18},{7,26},{10,23},{11,31},{14,19},{15,27},{16,4}... | collective-permute-start | bytes 2457608 | tf_op jit(solution)/shard_map/ppermute | solution.py:217
  512.1 49.8 %copy-start.12 = (f32[2,20,20,256]{3,0,2,1:T(2,128)}, f32[2,20,20,256]{3,0,2,1:T(2,128)S(1)}, u32[]{:S(2)}) copy-start(f32[2,20,20,256]{3,0,2,1:T(2,128)S(1)} %collective-permute-done.12) | copy-start | bytes 2457604
  512.2 56.4 %collective-permute-start.22 = (f32[2,20,20,256]{3,0,2,1:T(2,128)}, f32[2,20,20,256]{3,0,2,1:T(2,128)}, u32[]{:S(2)}, u32[]{:S(2)}) collective-permute-start(f32[2,20,20,256]{3,0,2,1:T(2,128)} %bitcast.114), channel_id=1, source_target_pairs={{0,4},{1,12},{4,0},{5,8},{8,5},{9,13},{12,1},{13,9},{18,22},{19,30... | collective-permute-start | bytes 2457608 | tf_op jit(solution)/shard_map/ppermute | solution.py:218
  518.3 7.0 %copy-start.10 = (f32[2,20,20,256]{3,0,2,1:T(2,128)}, f32[2,20,20,256]{3,0,2,1:T(2,128)S(1)}, u32[]{:S(2)}) copy-start(f32[2,20,20,256]{3,0,2,1:T(2,128)S(1)} %collective-permute-done.15) | copy-start | bytes 2457604
  518.3 56.9 %collective-permute-start.23 = (f32[2,20,20,256]{3,0,2,1:T(2,128)S(1)}, f32[2,20,20,256]{3,0,2,1:T(2,128)}, u32[]{:S(2)}, u32[]{:S(2)}) collective-permute-start(f32[2,20,20,256]{3,0,2,1:T(2,128)S(1)} %bitcast.139), channel_id=1, source_target_pairs={{2,0},{3,1},{6,4},{7,5},{10,8},{11,9},{14,12},{15,13},{16,18},{17,... | collective-permute-start | bytes 2457608 | tf_op jit(solution)/shard_map/ppermute | solution.py:217
  519.7 42.3 %copy-start.16 = (f32[2,20,20,256]{3,0,2,1:T(2,128)}, f32[2,20,20,256]{3,0,2,1:T(2,128)S(1)}, u32[]{:S(2)}) copy-start(f32[2,20,20,256]{3,0,2,1:T(2,128)S(1)} %collective-permute-done.17) | copy-start | bytes 2457604
  519.7 56.8 %collective-permute-start.25 = (f32[2,20,20,256]{3,0,2,1:T(2,128)S(1)}, f32[2,20,20,256]{3,0,2,1:T(2,128)}, u32[]{:S(2)}, u32[]{:S(2)}) collective-permute-start(f32[2,20,20,256]{3,0,2,1:T(2,128)S(1)} %bitcast.140), channel_id=1, source_target_pairs={{0,0},{1,8},{4,4},{5,12},{8,1},{9,9},{12,5},{13,13},{18,18},{19,26... | collective-permute-start | bytes 2457608 | tf_op jit(solution)/shard_map/ppermute | solution.py:218
  524.1 37.9 %copy-start.14 = (f32[2,20,20,256]{3,0,2,1:T(2,128)}, f32[2,20,20,256]{3,0,2,1:T(2,128)S(1)}, u32[]{:S(2)}) copy-start(f32[2,20,20,256]{3,0,2,1:T(2,128)S(1)} %collective-permute-done.19) | copy-start | bytes 2457604
  524.1 65.6 %collective-permute-start.26 = (f32[2,20,20,256]{3,0,2,1:T(2,128)}, f32[2,20,20,256]{3,0,2,1:T(2,128)}, u32[]{:S(2)}, u32[]{:S(2)}) collective-permute-start(f32[2,20,20,256]{3,0,2,1:T(2,128)} %bitcast.112), channel_id=1, source_target_pairs={{2,22},{3,30},{6,18},{7,26},{10,23},{11,31},{14,19},{15,27},{16,4}... | collective-permute-start | bytes 2457608 | tf_op jit(solution)/shard_map/ppermute | solution.py:217
  562.0 0.9 copy-start.18
  562.9 28.1 %collective-permute-start.28 = (f32[2,20,20,256]{3,0,2,1:T(2,128)}, f32[2,20,20,256]{3,0,2,1:T(2,128)}, u32[]{:S(2)}, u32[]{:S(2)}) collective-permute-start(f32[2,20,20,256]{3,0,2,1:T(2,128)} %bitcast.112), channel_id=1, source_target_pairs={{0,4},{1,12},{4,0},{5,8},{8,5},{9,13},{12,1},{13,9},{18,22},{19,30... | collective-permute-start | bytes 2457608 | tf_op jit(solution)/shard_map/ppermute | solution.py:218
  565.4 3.1 copy-start.17
  565.4 5.4 copy-start
  565.4 5.5 copy-start.2
  565.4 5.5 copy-start.4
  568.5 47.3 %collective-permute-start.18 = (f32[2,20,20,256]{3,0,2,1:T(2,128)S(1)}, f32[2,20,20,256]{3,0,2,1:T(2,128)S(1)}, u32[]{:S(2)}, u32[]{:S(2)}) collective-permute-start(f32[2,20,20,256]{3,0,2,1:T(2,128)S(1)} %copy-done.17), channel_id=1, source_target_pairs={{0,16},{1,24},{4,20},{5,28},{8,17},{9,25},{12,21},{13,29},{18,2},{... | collective-permute-start | bytes 2457608 | tf_op jit(solution)/shard_map/ppermute | solution.py:217
  570.9 5.6 copy-start.19
  570.9 9.7 %copy-start.9 = (f32[2,20,20,256]{3,0,2,1:T(2,128)S(1)}, f32[2,20,20,256]{3,0,2,1:T(2,128)}, u32[]{:S(2)}) copy-start(f32[2,20,20,256]{3,0,2,1:T(2,128)} %copy-done.8) | copy-start | bytes 2457604
  570.9 9.7 %copy-start.13 = (f32[2,20,20,256]{3,0,2,1:T(2,128)S(1)}, f32[2,20,20,256]{3,0,2,1:T(2,128)}, u32[]{:S(2)}) copy-start(f32[2,20,20,256]{3,0,2,1:T(2,128)} %copy-done.12) | copy-start | bytes 2457604
  570.9 33.4 %copy-start.7 = (f32[2,20,20,256]{3,0,2,1:T(2,128)S(1)}, f32[2,20,20,256]{3,0,2,1:T(2,128)}, u32[]{:S(2)}) copy-start(f32[2,20,20,256]{3,0,2,1:T(2,128)} %copy-done.6) | copy-start | bytes 2457604
  570.9 33.4 %copy-start.11 = (f32[2,20,20,256]{3,0,2,1:T(2,128)S(1)}, f32[2,20,20,256]{3,0,2,1:T(2,128)}, u32[]{:S(2)}) copy-start(f32[2,20,20,256]{3,0,2,1:T(2,128)} %copy-done.10) | copy-start | bytes 2457604
  570.9 52.3 %copy-start.15 = (f32[2,20,20,256]{3,0,2,1:T(2,128)S(1)}, f32[2,20,20,256]{3,0,2,1:T(2,128)}, u32[]{:S(2)}) copy-start(f32[2,20,20,256]{3,0,2,1:T(2,128)} %copy-done.14) | copy-start | bytes 2457604
  575.2 48.5 %collective-permute-start.29 = (f32[2,20,20,256]{3,0,2,1:T(2,128)S(1)}, f32[2,20,20,256]{3,0,2,1:T(2,128)S(1)}, u32[]{:S(2)}, u32[]{:S(2)}) collective-permute-start(f32[2,20,20,256]{3,0,2,1:T(2,128)S(1)} %bitcast.135), channel_id=1, source_target_pairs={{2,0},{3,1},{6,4},{7,5},{10,8},{11,9},{14,12},{15,13},{16,18},{17,... | collective-permute-start | bytes 2457608 | tf_op jit(solution)/shard_map/ppermute | solution.py:217
  576.5 49.1 %collective-permute-start.21 = (f32[2,20,20,256]{3,0,2,1:T(2,128)S(1)}, f32[2,20,20,256]{3,0,2,1:T(2,128)S(1)}, u32[]{:S(2)}, u32[]{:S(2)}) collective-permute-start(f32[2,20,20,256]{3,0,2,1:T(2,128)S(1)} %copy-done.19), channel_id=1, source_target_pairs={{22,20},{30,28},{18,16},{26,24},{23,21},{31,29},{19,17},{27,25},{4... | collective-permute-start | bytes 2457608 | tf_op jit(solution)/shard_map/ppermute | solution.py:217
  589.7 38.9 %collective-permute-start.32 = (f32[2,20,20,256]{3,0,2,1:T(2,128)S(1)}, f32[2,20,20,256]{3,0,2,1:T(2,128)S(1)}, u32[]{:S(2)}, u32[]{:S(2)}) collective-permute-start(f32[2,20,20,256]{3,0,2,1:T(2,128)S(1)} %bitcast.133), channel_id=1, source_target_pairs={{2,22},{3,30},{6,18},{7,26},{10,23},{11,31},{14,19},{15,27},{16,4}... | collective-permute-start | bytes 2457608 | tf_op jit(solution)/shard_map/ppermute | solution.py:217
  591.0 42.6 %collective-permute-start.24 = (f32[2,20,20,256]{3,0,2,1:T(2,128)}, f32[2,20,20,256]{3,0,2,1:T(2,128)S(1)}, u32[]{:S(2)}, u32[]{:S(2)}) collective-permute-start(f32[2,20,20,256]{3,0,2,1:T(2,128)} %collective-permute-done.23), channel_id=1, source_target_pairs={{0,16},{1,24},{4,20},{5,28},{8,17},{9,25},{12,21},{13,29},{18,2},{... | collective-permute-start | bytes 2457608 | tf_op jit(solution)/shard_map/ppermute | solution.py:217
  615.8 21.2 %collective-permute-start.27 = (f32[2,20,20,256]{3,0,2,1:T(2,128)}, f32[2,20,20,256]{3,0,2,1:T(2,128)S(1)}, u32[]{:S(2)}, u32[]{:S(2)}) collective-permute-start(f32[2,20,20,256]{3,0,2,1:T(2,128)} %collective-permute-done.26), channel_id=1, source_target_pairs={{22,20},{30,28},{18,16},{26,24},{23,21},{31,29},{19,17},{27,25},{4... | collective-permute-start | bytes 2457608 | tf_op jit(solution)/shard_map/ppermute | solution.py:217
  623.7 14.9 %collective-permute-start.31 = (f32[2,20,20,256]{3,0,2,1:T(2,128)S(1)}, f32[2,20,20,256]{3,0,2,1:T(2,128)S(1)}, u32[]{:S(2)}, u32[]{:S(2)}) collective-permute-start(f32[2,20,20,256]{3,0,2,1:T(2,128)S(1)} %bitcast.136), channel_id=1, source_target_pairs={{0,0},{1,8},{4,4},{5,12},{8,1},{9,9},{12,5},{13,13},{18,18},{19,26... | collective-permute-start | bytes 2457608 | tf_op jit(solution)/shard_map/ppermute | solution.py:218
  625.7 24.0 %collective-permute-start.30 = (f32[2,20,20,256]{3,0,2,1:T(2,128)S(1)}, f32[2,20,20,256]{3,0,2,1:T(2,128)S(1)}, u32[]{:S(2)}, u32[]{:S(2)}) collective-permute-start(f32[2,20,20,256]{3,0,2,1:T(2,128)S(1)} %collective-permute-done.29), channel_id=1, source_target_pairs={{0,16},{1,24},{4,20},{5,28},{8,17},{9,25},{12,21},{13,29},{18,2},{... | collective-permute-start | bytes 2457608 | tf_op jit(solution)/shard_map/ppermute | solution.py:217
  628.6 27.6 %collective-permute-start.34 = (f32[2,20,20,256]{3,0,2,1:T(2,128)S(1)}, f32[2,20,20,256]{3,0,2,1:T(2,128)S(1)}, u32[]{:S(2)}, u32[]{:S(2)}) collective-permute-start(f32[2,20,20,256]{3,0,2,1:T(2,128)S(1)} %bitcast.134), channel_id=1, source_target_pairs={{0,4},{1,12},{4,0},{5,8},{8,5},{9,13},{12,1},{13,9},{18,22},{19,30... | collective-permute-start | bytes 2457608 | tf_op jit(solution)/shard_map/ppermute | solution.py:218
  633.6 22.7 %collective-permute-start.33 = (f32[2,20,20,256]{3,0,2,1:T(2,128)S(1)}, f32[2,20,20,256]{3,0,2,1:T(2,128)S(1)}, u32[]{:S(2)}, u32[]{:S(2)}) collective-permute-start(f32[2,20,20,256]{3,0,2,1:T(2,128)S(1)} %collective-permute-done.32), channel_id=1, source_target_pairs={{22,20},{30,28},{18,16},{26,24},{23,21},{31,29},{19,17},{27,25},{4... | collective-permute-start | bytes 2457608 | tf_op jit(solution)/shard_map/ppermute | solution.py:217
